TPU v7x, 1024 devices: a whole 8x8x8 slice. The times are simulated.
1024 devices in a mesh: gx: 16 (over y_hi, z), gy: 64 (over y_lo, x, core).
Axes of the slice: x: 8, y: 8 (y_hi: 2, y_lo: 4; y = y_hi * 4 + y_lo), z: 8, core: 2. Of those that a mesh axis runs over, the one named last changes fastest.
Arguments:
- air_state: float32 [512, 2048, 128], P('gx', 'gy'), may hold values from -3 to 4, as said below
- edge_map: int32 [16, 64, 4], replicated, may hold values from 0 to 7
- tile_class: int32 [16, 64, 16], P(None, 'gy'), may hold values from 0 to 1, as said below
- in_weight: bfloat16 [128, 1024], replicated, may hold values from -0.5 to 0.5
- in_bias: float32 [1024], replicated, may hold values from -4 to 4
- mid_weight: bfloat16 [1024, 1024], replicated, may hold values from -0.1875 to 0.1875
- mid_bias: float32 [1024], replicated, may hold values from -4 to 4
- out_weight: bfloat16 [1024, 128], replicated, may hold values from -0.1875 to 0.1875
- land_in: bfloat16 [128, 1024], replicated, may hold values from -0.5 to 0.5
- land_bias: float32 [1024], replicated, may hold values from -4 to 4
- land_out: bfloat16 [1024, 128], replicated, may hold values from -0.1875 to 0.1875
Outputs:
- tendency: float32 [512, 2048, 128], P('gx', 'gy')
Inputs may be any that keep to these rules, and one draw needn't show every extreme that they name: `air_state`: density lies in 0.5 to 2, the speeds (momentum over density) are at most 1.5 in magnitude and potential temperature lies in 0.5 to 2. For every gy index g and tile number t, exactly 4 of the devices d along gx have tile_class[d, g, t] = 1.
All inputs are finite; a program needn't handle non-finite values.
Results may differ from a plain program's by a relative error of at most 0.0024.
Values may be sent and summed in bfloat16 or wider, within the bound.
No kernel may reach another device: no remote copies, remote signals or barrier semaphores. Data moves between devices by JAX's collectives and lax.ppermute only.
A program may use at most 64 MiB of HBM per device.

v0:
```python
import math

import jax
import jax.numpy as jnp
import numpy as np
from jax import lax
from jax.sharding import PartitionSpec as P


def padded_2(x, sides, width):
    for axis, dim in sides:
        peers, length = (lax.axis_size(axis), x.shape[dim])
        up = [(i, (i + 1) % peers) for i in range(peers)]
        down = [(j, i) for i, j in up]
        last = lax.slice_in_dim(x, length - width, length, axis=dim)
        leading = lax.slice_in_dim(x, 0, width, axis=dim)
        before = lax.ppermute(last, axis, up)
        after = lax.ppermute(leading, axis, down)
        x = jnp.concatenate([before, x, after], axis=dim)
    return x


def lobatto_tables():
    points = np.array([-1.0, -math.sqrt(0.2), math.sqrt(0.2), 1.0])
    weights = [1.0 / 6.0, 5.0 / 6.0, 5.0 / 6.0, 1.0 / 6.0]
    barycentric = np.array(
        [1.0 / np.prod([points[j] - points[k] for k in range(4) if k != j]) for j in range(4)]
    )
    derivative = np.zeros((4, 4))
    for i in range(4):
        for j in range(4):
            if i != j:
                derivative[i, j] = barycentric[j] / barycentric[i] / (points[i] - points[j])
        derivative[i, i] = -np.sum([derivative[i, k] for k in range(4) if k != i])
    return (derivative, weights)


def primitives(states, direction):
    levels = states.shape[-1] // 4
    density = states[..., :levels]
    density_all = jnp.concatenate([density] * 4, axis=-1)
    carried = states / density_all
    velocity = carried[..., direction * levels : (direction + 1) * levels]
    velocity_all = jnp.concatenate([velocity] * 4, axis=-1)
    pressure = 0.5 * states[..., 3 * levels :]
    zero_block = jnp.zeros_like(pressure)
    pieces = [zero_block, zero_block, zero_block, zero_block]
    pieces[direction] = pressure
    pressure_all = jnp.concatenate(pieces, axis=-1)
    return (density_all, velocity_all, carried, pressure_all)


def two_point(state_one, state_two):
    return 0.125 * (state_one[0] + state_two[0]) * (state_one[1] + state_two[1]) * (
        state_one[2] + state_two[2]
    ) + 0.5 * (state_one[3] + state_two[3])


def directional(states, low_trace, high_trace, direction):
    derivative, weights = lobatto_tables()
    node_count, cross_count, features = states.shape
    elements = node_count // 4
    blocked = states.reshape(elements, 4, cross_count, features)
    node_prims = [primitives(blocked[:, a], direction) for a in range(4)]
    left_states = jnp.concatenate([low_trace[None], blocked[:, 3]], axis=0)
    right_states = jnp.concatenate([blocked[:, 0], high_trace[None]], axis=0)
    left_prims = primitives(left_states, direction)
    right_prims = primitives(right_states, direction)
    wave_speed = jnp.maximum(jnp.abs(left_prims[1]), jnp.abs(right_prims[1])) + 1.0
    face_flux = two_point(left_prims, right_prims) - 0.5 * wave_speed * (right_states - left_states)
    pair_flux = {}
    for a in range(4):
        for b in range(a, 4):
            pair_flux[a, b] = two_point(node_prims[a], node_prims[b])
    results = []
    for a in range(4):
        volume = jnp.zeros_like(pair_flux[0, 0])
        for b in range(4):
            key_pair = (a, b) if a <= b else (b, a)
            volume = volume + 2.0 * float(derivative[a, b]) * pair_flux[key_pair]
        result = -volume
        if a == 0:
            result = result + 1.0 / weights[0] * (face_flux[:-1] - pair_flux[0, 0])
        if a == 3:
            result = result - 1.0 / weights[3] * (face_flux[1:] - pair_flux[3, 3])
        results.append(result)
    return jnp.stack(results, axis=1).reshape(node_count, cross_count, features)


def device_dynamics(block, west_trace, east_trace, south_trace, north_trace):
    along_first = directional(block, west_trace, east_trace, 1)
    along_second = directional(block.transpose(1, 0, 2), south_trace, north_trace, 2).transpose(
        1, 0, 2
    )
    return along_first + along_second


def normalize(columns):
    values = columns.astype(jnp.float32)
    inverse_rms = lax.rsqrt(jnp.mean(values * values, axis=-1, keepdims=True) + 1e-06)
    return (values * inverse_rms).astype(jnp.bfloat16)


def main_branch(normed, in_weight, in_bias, out_weight):
    first_hidden = jax.nn.silu(
        jnp.dot(normed, in_weight, preferred_element_type=jnp.float32) + in_bias
    ).astype(jnp.bfloat16)
    return jnp.dot(first_hidden, out_weight, preferred_element_type=jnp.float32)


def land_branch(normed, land_in, land_bias, mid_weight, mid_bias, land_out):
    land_hidden = jax.nn.silu(
        jnp.dot(normed, land_in, preferred_element_type=jnp.float32) + land_bias
    ).astype(jnp.bfloat16)
    land_second = jax.nn.silu(
        jnp.dot(land_hidden, mid_weight, preferred_element_type=jnp.float32) + mid_bias
    ).astype(jnp.bfloat16)
    return jnp.dot(land_second, land_out, preferred_element_type=jnp.float32)


def oriented(candidates, edge_code):
    picked = lax.dynamic_index_in_dim(candidates, edge_code % 4, 0, keepdims=False)
    return jnp.where(edge_code >= 4, picked[::-1], picked)


def on_device(
    air_state,
    edge_map,
    tile_class,
    in_weight,
    in_bias,
    mid_weight,
    mid_bias,
    out_weight,
    land_in,
    land_bias,
    land_out,
):
    node_count = air_state.shape[0]
    features = air_state.shape[2]
    row_index = lax.axis_index("gx")
    column_index = lax.axis_index("gy")
    row_total = lax.axis_size("gx")
    own_edges = jnp.stack([air_state[0], air_state[-1], air_state[:, 0], air_state[:, -1]])
    padded = padded_2(own_edges[None, None], (("gx", 0), ("gy", 1)), 1)
    west_trace = oriented(padded[0, 1], edge_map[row_index, column_index, 0])
    east_trace = oriented(padded[2, 1], edge_map[row_index, column_index, 1])
    south_trace = oriented(padded[1, 0], edge_map[row_index, column_index, 2])
    north_trace = oriented(padded[1, 2], edge_map[row_index, column_index, 3])
    dynamics = device_dynamics(air_state, west_trace, east_trace, south_trace, north_trace)
    tile_columns = node_count * node_count // row_total
    group_classes = tile_class[:, 0, :]
    own_class = lax.dynamic_index_in_dim(group_classes, row_index, 0, keepdims=False)
    land_weight = jnp.repeat(
        own_class, tile_columns, total_repeat_length=row_total * tile_columns
    ).astype(jnp.float32)[:, None]
    normed = normalize(air_state.reshape(-1, features).astype(jnp.bfloat16))
    base_term = main_branch(normed, in_weight, in_bias, out_weight)
    land_term = land_branch(normed, land_in, land_bias, mid_weight, mid_bias, land_out)
    physics = (
        (base_term + land_weight * land_term)
        .astype(jnp.bfloat16)
        .reshape(node_count, node_count, features)
    )
    return dynamics + physics.astype(jnp.float32)


def solution(mesh):
    return jax.shard_map(
        on_device,
        mesh=mesh,
        in_specs=(
            P("gx", "gy", None),
            P(),
            P(None, "gy", None),
            P(),
            P(),
            P(),
            P(),
            P(),
            P(),
            P(),
            P(),
        ),
        out_specs=P("gx", "gy", None),
        check_vma=False,
    )
```

profile of v0, /device:TPU:16, one launch (start us, length us, event | category | flops | bytes accessed | tf_op | source)
XLA Modules:
  0.0 135.7 jit_solution(4999301940434887306)
XLA Ops:
  0.0 1.1 fusion.70
  2.5 5.2 %collective-permute-start = (f32[1,1,4,32,128]{4,3,2,1,0:T(8,128)}, f32[1,1,4,32,128]{4,3,2,1,0:T(8,128)}, u32[]{:S(2)}, u32[]{:S(2)}) collective-permute-start(f32[1,1,4,32,128]{4,3,2,1,0:T(8,128)} %maximum_bitcast_fusion), channel_id=1, source_target_pairs={{0,64},{64,128},{128,192},{192,256},{256,320},{320,384},{384,448},... | collective-permute-start | bytes 196616 | tf_op jit(solution)/shard_map/ppermute | solution.py:17
  7.7 18.9 %collective-permute-start.1 = (f32[1,1,4,32,128]{4,3,2,1,0:T(8,128)}, f32[1,1,4,32,128]{4,3,2,1,0:T(8,128)}, u32[]{:S(2)}, u32[]{:S(2)}) collective-permute-start(f32[1,1,4,32,128]{4,3,2,1,0:T(8,128)} %maximum_bitcast_fusion), channel_id=1, source_target_pairs={{64,0},{128,64},{192,128},{256,192},{320,256},{384,320},{448,384},... | collective-permute-start | bytes 196616 | tf_op jit(solution)/shard_map/ppermute | solution.py:18
  26.6 1.1 fusion.67
  35.0 1.8 %add_negate_fusion.3 = f32[8,1,32,128]{3,0,2,1:T(8,128)} fusion(f32[8,1,32,128]{3,2,1,0:T(8,128)S(1)} %get-tuple-element.30, f32[8,1,32,128]{3,2,1,0:T(8,128)S(1)} %get-tuple-element.29, f32[8,1,32,128]{3,2,1,0:T(8,128)S(1)} %get-tuple-element.28, f32[8,1,32,128]{3,2,1,0:T(8,128)S(1)} %get-tuple-element.31, f32[8,1,32,64]{3,0,2,1:T(8,128)S(1)} %concatenate.737, ...), kind=kLoop, calls=%fused_computation.173 | loop fusion | flops 2621440 | bytes 1146880 | tf_op jit(solution)/shard_map/neg | solution.py:81
  36.7 1.8 %add_negate_fusion.2 = f32[8,1,32,128]{3,0,2,1:T(8,128)} fusion(f32[8,1,32,128]{3,2,1,0:T(8,128)S(1)} %get-tuple-element.30, f32[8,1,32,128]{3,2,1,0:T(8,128)S(1)} %get-tuple-element.29, f32[8,1,32,128]{3,2,1,0:T(8,128)S(1)} %get-tuple-element.28, f32[8,1,32,128]{3,2,1,0:T(8,128)S(1)} %get-tuple-element.31, f32[8,1,32,64]{3,0,2,1:T(8,128)S(1)} %concatenate.737, ...), kind=kLoop, calls=%fused_computation.172 | loop fusion | flops 2621440 | bytes 1146880 | tf_op jit(solution)/shard_map/neg | solution.py:81
  39.0 0.9 multiply_reduce_fusion
  39.9 2.4 %fusion.68 = (f32[8,1,32,128]{3,1,0,2:T(1,128)S(1)}, f32[8,1,32,128]{3,1,0,2:T(1,128)S(1)}, f32[8,1,32,128]{3,1,0,2:T(1,128)S(1)}, f32[8,1,32,128]{3,1,0,2:T(1,128)S(1)}) fusion(f32[8,4,32,128]{3,1,0,2:T(4,128)} %bitcast.215), kind=kLoop, calls=%fused_computation.258 | loop fusion | bytes 1048576 | tf_op jit(solution)/shard_map/slice | solution.py:64
  53.7 4.9 %compare_select_fusion.1 = (s32[1024,1]{0,1:T(1,128)}, s32[1024,1]{0,1:T(1,128)S(1)}) fusion(s32[]{:T(128)} %bitcast.75, s32[]{:T(128)} %bitcast.76, s32[]{:T(128)} %bitcast.77, s32[]{:T(128)} %bitcast.78, s32[]{:T(128)} %bitcast.79, s32[]{:T(128)} %bitcast.81, s32[]{:T(128)} %bitcast.80, s32[1024,1]{0,1:T(1,128)S(1)} %bitcast.237, s32[1024,1]{0,1:T(1,128)S(1)} %bitcast.236), kind=kLoop, calls=%fused_computation.210 | loop fusion | flops 14336 | bytes 16412 | tf_op jit(solution)/shard_map/jit(_take)/gather | solution.py:154
  60.7 1.9 %slice_bitcast_fusion = (f32[8,1,32,32]{3,0,2,1:T(8,128)}, f32[8,32,32]{2,0,1:T(8,128)}, f32[8,32,32]{2,0,1:T(8,128)}, f32[8,1,32,32]{3,0,2,1:T(8,128)}) fusion(f32[8,32,128]{2,0,1:T(8,128)} %fusion.48, f32[8,32,128]{2,0,1:T(8,128)} %fusion.49), kind=kLoop, calls=%fused_computation.233 | loop fusion | bytes 196608 | tf_op jit(solution)/shard_map/concatenate | solution.py:44
  62.7 1.9 %slice_bitcast_fusion.4 = (f32[8,1,32,32]{3,0,2,1:T(8,128)}, f32[8,32,32]{2,0,1:T(8,128)}, f32[8,32,32]{2,0,1:T(8,128)}, f32[8,1,32,32]{3,0,2,1:T(8,128)}) fusion(f32[8,32,128]{2,0,1:T(8,128)} %fusion.50, f32[8,32,128]{2,0,1:T(8,128)} %fusion.51), kind=kLoop, calls=%fused_computation.237 | loop fusion | bytes 196608 | tf_op jit(solution)/shard_map/concatenate | solution.py:44
  64.5 1.2 fusion.7
  66.0 2.6 %multiply_convert_fusion.1 = bf16[1024,1024]{1,0:T(8,128)(2,1)} fusion(bf16[1024,128]{1,0:T(8,128)(2,1)S(1)} %fusion.7, bf16[128,1024]{1,0:T(8,128)(2,1)S(1)} %copy-done.73, f32[1024]{0:T(1024)S(1)} %copy-done.74), kind=kOutput, calls=%fused_computation.1 | convolution fusion | flops 274726912 | bytes 2625536 | tf_op jit(solution)/shard_map/dot_general | solution.py:113
  68.7 5.7 %fusion.56 = f32[1024]{0:T(1024)S(1)} fusion(pred[1024]{0:T(1024)(128)(4,1)S(1)} %copy-done.71, pred[1024]{0:T(1024)(128)(4,1)S(1)} %copy-done.70, pred[1024]{0:T(1024)(128)(4,1)S(1)} %copy-done.69, pred[1024]{0:T(1024)(128)(4,1)S(1)} %copy-done.68, pred[1024]{0:T(1024)(128)(4,1)S(1)} %copy-done.67, pred[1024]{0:T(1024)(128)(4,1)S(1)} %copy-done.66, ...), kind=kLoop, calls=%fused_computation.224 | loop fusion | flops 19456 | bytes 21572 | tf_op jit(solution)/shard_map/convert_element_type | solution.py:156
  74.3 5.4 %fusion.5 = f32[1024,128]{1,0:T(8,128)} fusion(bf16[1024,128]{1,0:T(8,128)(2,1)} %param.23, f32[1024]{0:T(1024)S(1)} %copy-done.75, bf16[1024,1024]{1,0:T(8,128)(2,1)} %multiply_convert_fusion.1, bf16[1024,1024]{1,0:T(8,128)(2,1)S(1)} %copy-done, f32[1024]{0:T(1024)S(1)} %fusion.56), kind=kOutput, calls=%fused_computation.7 | convolution fusion | flops 2422341632 | bytes 4988928 | tf_op jit(solution)/shard_map/dot_general | solution.py:118
  79.8 3.7 %fusion.6 = bf16[1024,128]{1,0:T(8,128)(2,1)} fusion(f32[1024,128]{1,0:T(8,128)} %fusion.5, bf16[1024,128]{1,0:T(8,128)(2,1)} %param.20, bf16[1024,128]{1,0:T(8,128)(2,1)} %copy-done.60, bf16[128,1024]{1,0:T(8,128)(2,1)} %param.16, f32[1024]{0:T(1024)S(1)} %copy-done.76), kind=kOutput, calls=%fused_computation.8 | convolution fusion | flops 543424512 | bytes 1576960 | tf_op jit(solution)/shard_map/dot_general | solution.py:108
  83.6 4.8 %add_negate_fusion.1 = f32[8,1,32,128]{3,0,2,1:T(8,128)} fusion(f32[8,1,32,128]{3,0,2,1:T(8,128)S(1)} %bitcast.210, f32[8,1,32,32]{3,0,2,1:T(8,128)S(1)} %concatenate.735, f32[8,1,32,32]{3,0,2,1:T(8,128)} %get-tuple-element.75, f32[8,1,32,64]{3,0,2,1:T(8,128)} %copy-done.2, f32[8,1,32,32]{3,0,2,1:T(8,128)} %get-tuple-element.87, ...), kind=kLoop, calls=%fused_computation.169 | loop fusion | flops 2621440 | bytes 1146880 | tf_op jit(solution)/shard_map/neg | solution.py:81
  88.5 1.7 %add_negate_fusion = f32[8,1,32,128]{3,0,2,1:T(8,128)} fusion(f32[8,1,32,128]{3,0,2,1:T(8,128)S(1)} %bitcast.211, f32[8,1,32,32]{3,0,2,1:T(8,128)S(1)} %concatenate.735, f32[8,1,32,32]{3,0,2,1:T(8,128)S(1)} %copy-done.46, f32[8,1,32,64]{3,0,2,1:T(8,128)S(1)} %copy-done.3, f32[8,1,32,32]{3,0,2,1:T(8,128)S(1)} %copy-done.48, ...), kind=kLoop, calls=%fused_computation.168 | loop fusion | flops 2621440 | bytes 1146880 | tf_op jit(solution)/shard_map/neg | solution.py:81
  90.2 1.5 %constant_dynamic-slice_fusion.3 = (s32[1,1,1]{1,2,0:T(1,128)}, s32[1,1,1]{1,2,0:T(1,128)}, s32[1,1,1]{1,2,0:T(1,128)}, s32[1,1,1]{1,2,0:T(1,128)}) fusion(s32[16,64,4]{1,2,0:T(4,128)} %param.14, s32[]{:T(128)S(6)} %select_n.101, s32[]{:T(128)S(6)} %select_n.102), kind=kLoop, calls=%fused_computation.229 | loop fusion | bytes 40 | tf_op jit(solution)/shard_map/dynamic_slice | solution.py:147
  103.3 0.9 fusion.27
  108.2 1.8 %pad_maximum_fusion.54 = f32[3,1,4,32,128]{4,3,2,1,0:T(8,128)} fusion(f32[1,1,4,32,128]{4,3,2,1,0:T(8,128)} %collective-permute-done.1, f32[1,1,4,32,128]{4,3,2,1,0:T(8,128)} %maximum_bitcast_fusion, f32[1,1,4,32,128]{4,3,2,1,0:T(8,128)} %collective-permute-done), kind=kLoop, calls=%fused_computation.113 | loop fusion | flops 98304 | bytes 393216 | tf_op jit(solution)/shard_map/concatenate | solution.py:19
  110.0 4.6 %collective-permute-start.3 = (f32[3,1,4,32,128]{4,3,2,1,0:T(8,128)}, f32[3,1,4,32,128]{4,3,2,1,0:T(8,128)S(1)}, u32[]{:S(2)}, u32[]{:S(2)}) collective-permute-start(f32[3,1,4,32,128]{4,3,2,1,0:T(8,128)} %pad_maximum_fusion.54), channel_id=1, source_target_pairs={{1,0},{2,1},{3,2},{4,3},{5,4},{6,5},{7,6},{8,7},{9,8},{10,9},{11,1... | collective-permute-start | bytes 589832 | tf_op jit(solution)/shard_map/ppermute | solution.py:18
  114.8 1.1 fusion.15
  116.0 1.1 fusion.42
  117.2 1.1 fusion.45
  118.3 1.9 %collective-permute-start.2 = (f32[3,1,4,32,128]{4,3,2,1,0:T(8,128)}, f32[3,1,4,32,128]{4,3,2,1,0:T(8,128)}, u32[]{:S(2)}, u32[]{:S(2)}) collective-permute-start(f32[3,1,4,32,128]{4,3,2,1,0:T(8,128)} %pad_maximum_fusion.54), channel_id=1, source_target_pairs={{0,1},{1,2},{2,3},{3,4},{4,5},{5,6},{6,7},{7,8},{8,9},{9,10},{10,1... | collective-permute-start | bytes 589832 | tf_op jit(solution)/shard_map/ppermute | solution.py:17
  120.3 0.9 copy.17
  121.2 6.5 %collective-permute-done.2 = f32[3,1,4,32,128]{4,3,2,1,0:T(8,128)} collective-permute-done((f32[3,1,4,32,128]{4,3,2,1,0:T(8,128)}, f32[3,1,4,32,128]{4,3,2,1,0:T(8,128)}, u32[]{:S(2)}, u32[]{:S(2)}) %collective-permute-start.2) | collective-permute-done | bytes 196640 | tf_op jit(solution)/shard_map/ppermute | solution.py:17
  129.8 2.1 %fusion.17 = f32[9,32,128]{2,0,1:T(8,128)S(1)} fusion(f32[8,32,128]{2,0,1:T(8,128)S(1)} %bitcast.199, f32[1,32,128]{2,0,1:T(1,128)S(1)} %bitcast.227, f32[1,32,128]{2,0,1:T(1,128)S(1)} %bitcast.224, f32[8,32,128]{2,0,1:T(8,128)S(1)} %bitcast.190, f32[9,32,32]{2,0,1:T(8,128)} %copy-done.6, f32[9,32,64]{2,0,1:T(8,128)} %copy-done.7, ...), kind=kLoop, calls=%fused_computation.85 | loop fusion | flops 1363968 | bytes 774144 | tf_op jit(solution)/shard_map/sub | solution.py:70
  132.1 1.1 fusion.39
  133.2 1.1 fusion.37
  134.8 0.9 convert_add_fusion
  (220 shorter events, 30.9 us)
Async XLA Ops:
  0.0 74.3 %copy-start = (bf16[1024,1024]{1,0:T(8,128)(2,1)S(1)}, bf16[1024,1024]{1,0:T(8,128)(2,1)}, u32[]{:S(2)}) copy-start(bf16[1024,1024]{1,0:T(8,128)(2,1)} %param.18) | copy-start | bytes 6291460
  2.5 99.3 %collective-permute-start = (f32[1,1,4,32,128]{4,3,2,1,0:T(8,128)}, f32[1,1,4,32,128]{4,3,2,1,0:T(8,128)}, u32[]{:S(2)}, u32[]{:S(2)}) collective-permute-start(f32[1,1,4,32,128]{4,3,2,1,0:T(8,128)} %maximum_bitcast_fusion), channel_id=1, source_target_pairs={{0,64},{64,128},{128,192},{192,256},{256,320},{320,384},{384,448},... | collective-permute-start | bytes 196616 | tf_op jit(solution)/shard_map/ppermute | solution.py:17
  7.7 98.3 %collective-permute-start.1 = (f32[1,1,4,32,128]{4,3,2,1,0:T(8,128)}, f32[1,1,4,32,128]{4,3,2,1,0:T(8,128)}, u32[]{:S(2)}, u32[]{:S(2)}) collective-permute-start(f32[1,1,4,32,128]{4,3,2,1,0:T(8,128)} %maximum_bitcast_fusion), channel_id=1, source_target_pairs={{64,0},{128,64},{192,128},{256,192},{320,256},{384,320},{448,384},... | collective-permute-start | bytes 196616 | tf_op jit(solution)/shard_map/ppermute | solution.py:18
  59.9 5.9 %copy-start.74 = (f32[1024]{0:T(1024)S(1)}, f32[1024]{0:T(1024)}, u32[]{:S(2)}) copy-start(f32[1024]{0:T(1024)} %param.22) | copy-start | bytes 12292
  60.7 5.1 %copy-start.73 = (bf16[128,1024]{1,0:T(8,128)(2,1)S(1)}, bf16[128,1024]{1,0:T(8,128)(2,1)}, u32[]{:S(2)}) copy-start(bf16[128,1024]{1,0:T(8,128)(2,1)} %param.21) | copy-start | bytes 786436
  65.9 8.4 %copy-start.75 = (f32[1024]{0:T(1024)S(1)}, f32[1024]{0:T(1024)}, u32[]{:S(2)}) copy-start(f32[1024]{0:T(1024)} %param.19) | copy-start | bytes 12292
  74.3 5.4 %copy-start.76 = (f32[1024]{0:T(1024)S(1)}, f32[1024]{0:T(1024)}, u32[]{:S(2)}) copy-start(f32[1024]{0:T(1024)} %param.17) | copy-start | bytes 12292
  83.5 4.9 %copy-start.44 = (f32[8,1,32,32]{3,0,2,1:T(8,128)S(1)}, f32[8,1,32,32]{3,0,2,1:T(8,128)}, u32[]{:S(2)}) copy-start(f32[8,1,32,32]{3,0,2,1:T(8,128)} %get-tuple-element.83) | copy-start | bytes 98308
  83.5 4.9 %copy-start.45 = (f32[8,1,32,32]{3,0,2,1:T(8,128)S(1)}, f32[8,1,32,32]{3,0,2,1:T(8,128)}, u32[]{:S(2)}) copy-start(f32[8,1,32,32]{3,0,2,1:T(8,128)} %get-tuple-element.74) | copy-start | bytes 98308
  83.5 4.9 %copy-start.46 = (f32[8,1,32,32]{3,0,2,1:T(8,128)S(1)}, f32[8,1,32,32]{3,0,2,1:T(8,128)}, u32[]{:S(2)}) copy-start(f32[8,1,32,32]{3,0,2,1:T(8,128)} %get-tuple-element.75) | copy-start | bytes 98308
  83.5 4.9 %copy-start.47 = (f32[8,1,32,32]{3,0,2,1:T(8,128)S(1)}, f32[8,1,32,32]{3,0,2,1:T(8,128)}, u32[]{:S(2)}) copy-start(f32[8,1,32,32]{3,0,2,1:T(8,128)} %get-tuple-element.86) | copy-start | bytes 98308
  83.6 4.9 %copy-start.48 = (f32[8,1,32,32]{3,0,2,1:T(8,128)S(1)}, f32[8,1,32,32]{3,0,2,1:T(8,128)}, u32[]{:S(2)}) copy-start(f32[8,1,32,32]{3,0,2,1:T(8,128)} %get-tuple-element.87) | copy-start | bytes 98308
  83.6 4.9 %copy-start.49 = (f32[8,1,32,32]{3,0,2,1:T(8,128)S(1)}, f32[8,1,32,32]{3,0,2,1:T(8,128)}, u32[]{:S(2)}) copy-start(f32[8,1,32,32]{3,0,2,1:T(8,128)} %get-tuple-element.96) | copy-start | bytes 98308
  83.6 4.9 %copy-start.50 = (f32[8,1,32,32]{3,0,2,1:T(8,128)S(1)}, f32[8,1,32,32]{3,0,2,1:T(8,128)}, u32[]{:S(2)}) copy-start(f32[8,1,32,32]{3,0,2,1:T(8,128)} %get-tuple-element.127) | copy-start | bytes 98308
  83.6 4.9 %copy-start.51 = (f32[8,1,32,32]{3,0,2,1:T(8,128)S(1)}, f32[8,1,32,32]{3,0,2,1:T(8,128)}, u32[]{:S(2)}) copy-start(f32[8,1,32,32]{3,0,2,1:T(8,128)} %get-tuple-element.92) | copy-start | bytes 98308
  106.7 8.0 %copy-start.5 = (f32[9,32,32]{2,0,1:T(8,128)S(1)}, f32[9,32,32]{2,0,1:T(8,128)}, u32[]{:S(2)}) copy-start(f32[9,32,32]{2,0,1:T(8,128)} %copy-done.4) | copy-start | bytes 110596
  106.7 8.0 %copy-start.53 = (f32[9,32,32]{2,0,1:T(8,128)S(1)}, f32[9,32,32]{2,0,1:T(8,128)}, u32[]{:S(2)}) copy-start(f32[9,32,32]{2,0,1:T(8,128)} %slice.290) | copy-start | bytes 110596
  106.8 8.0 %copy-start.54 = (f32[9,32,32]{2,0,1:T(8,128)S(1)}, f32[9,32,32]{2,0,1:T(8,128)}, u32[]{:S(2)}) copy-start(f32[9,32,32]{2,0,1:T(8,128)} %get-tuple-element.43) | copy-start | bytes 110596
  108.0 7.9 %copy-start.12 = (f32[8,32,32]{2,0,1:T(8,128)S(1)}, f32[8,32,32]{2,0,1:T(8,128)}, u32[]{:S(2)}) copy-start(f32[8,32,32]{2,0,1:T(8,128)} %copy-done.11) | copy-start | bytes 98308
  108.0 7.9 %copy-start.20 = (f32[8,32,32]{2,0,1:T(8,128)S(1)}, f32[8,32,32]{2,0,1:T(8,128)}, u32[]{:S(2)}) copy-start(f32[8,32,32]{2,0,1:T(8,128)} %copy-done.19) | copy-start | bytes 98308
  108.0 7.9 %copy-start.22 = (f32[8,32,32]{2,0,1:T(8,128)S(1)}, f32[8,32,32]{2,0,1:T(8,128)}, u32[]{:S(2)}) copy-start(f32[8,32,32]{2,0,1:T(8,128)} %copy-done.21) | copy-start | bytes 98308
  108.0 7.9 %copy-start.24 = (f32[8,32,32]{2,0,1:T(8,128)S(1)}, f32[8,32,32]{2,0,1:T(8,128)}, u32[]{:S(2)}) copy-start(f32[8,32,32]{2,0,1:T(8,128)} %copy-done.23) | copy-start | bytes 98308
  108.0 7.9 %copy-start.25 = (f32[8,32,32]{2,0,1:T(8,128)S(1)}, f32[8,32,32]{2,0,1:T(8,128)}, u32[]{:S(2)}) copy-start(f32[8,32,32]{2,0,1:T(8,128)} %get-tuple-element.59) | copy-start | bytes 98308
  108.0 7.9 %copy-start.26 = (f32[8,32,32]{2,0,1:T(8,128)S(1)}, f32[8,32,32]{2,0,1:T(8,128)}, u32[]{:S(2)}) copy-start(f32[8,32,32]{2,0,1:T(8,128)} %get-tuple-element.73) | copy-start | bytes 98308
  108.0 7.9 %copy-start.27 = (f32[8,32,32]{2,0,1:T(8,128)S(1)}, f32[8,32,32]{2,0,1:T(8,128)}, u32[]{:S(2)}) copy-start(f32[8,32,32]{2,0,1:T(8,128)} %get-tuple-element.61) | copy-start | bytes 98308
  108.1 7.9 %copy-start.28 = (f32[8,32,32]{2,0,1:T(8,128)S(1)}, f32[8,32,32]{2,0,1:T(8,128)}, u32[]{:S(2)}) copy-start(f32[8,32,32]{2,0,1:T(8,128)} %get-tuple-element.67) | copy-start | bytes 98308
  108.1 7.9 %copy-start.30 = (f32[8,32,32]{2,0,1:T(8,128)S(1)}, f32[8,32,32]{2,0,1:T(8,128)}, u32[]{:S(2)}) copy-start(f32[8,32,32]{2,0,1:T(8,128)} %get-tuple-element.52) | copy-start | bytes 98308
  108.1 7.9 %copy-start.34 = (f32[8,32,32]{2,0,1:T(8,128)S(1)}, f32[8,32,32]{2,0,1:T(8,128)}, u32[]{:S(2)}) copy-start(f32[8,32,32]{2,0,1:T(8,128)} %get-tuple-element.70) | copy-start | bytes 98308
  108.1 7.9 %copy-start.35 = (f32[8,32,32]{2,0,1:T(8,128)S(1)}, f32[8,32,32]{2,0,1:T(8,128)}, u32[]{:S(2)}) copy-start(f32[8,32,32]{2,0,1:T(8,128)} %get-tuple-element.56) | copy-start | bytes 98308
  108.1 7.9 %copy-start.36 = (f32[8,32,32]{2,0,1:T(8,128)S(1)}, f32[8,32,32]{2,0,1:T(8,128)}, u32[]{:S(2)}) copy-start(f32[8,32,32]{2,0,1:T(8,128)} %get-tuple-element.64) | copy-start | bytes 98308
  110.0 11.1 %collective-permute-start.3 = (f32[3,1,4,32,128]{4,3,2,1,0:T(8,128)}, f32[3,1,4,32,128]{4,3,2,1,0:T(8,128)S(1)}, u32[]{:S(2)}, u32[]{:S(2)}) collective-permute-start(f32[3,1,4,32,128]{4,3,2,1,0:T(8,128)} %pad_maximum_fusion.54), channel_id=1, source_target_pairs={{1,0},{2,1},{3,2},{4,3},{5,4},{6,5},{7,6},{8,7},{9,8},{10,9},{11,1... | collective-permute-start | bytes 589832 | tf_op jit(solution)/shard_map/ppermute | solution.py:18
  118.3 9.4 %collective-permute-start.2 = (f32[3,1,4,32,128]{4,3,2,1,0:T(8,128)}, f32[3,1,4,32,128]{4,3,2,1,0:T(8,128)}, u32[]{:S(2)}, u32[]{:S(2)}) collective-permute-start(f32[3,1,4,32,128]{4,3,2,1,0:T(8,128)} %pad_maximum_fusion.54), channel_id=1, source_target_pairs={{0,1},{1,2},{2,3},{3,4},{4,5},{5,6},{6,7},{7,8},{8,9},{9,10},{10,1... | collective-permute-start | bytes 589832 | tf_op jit(solution)/shard_map/ppermute | solution.py:17
  (49 other events, 138.0 us)
where the time goes:
time: 137 us; the launch traced here: 136 us
  other arithmetic  51.1 us (37%)
  starting transfers between devices  30.6 us (22%)
  local copies, waits for them, and re-layouts  24.4 us (18%)
  matrix products  11.8 us (9%)
  between operations  11.4 us (8%)
  waiting for transfers between devices  6.5 us (5%)
    ppermute x2, starting transfers between devices, padded_2(): after = lax.ppermute(leading, axis, down)  23.5 us
    neg x4, other arithmetic, directional(): result = -volume  10 us
    ppermute x2, starting transfers between devices, padded_2(): before = lax.ppermute(last, axis, up)  7.1 us
    concatenate x6, local copies, waits for them, and re-layouts, primitives(): velocity_all = jnp.concatenate([velocity] * 4, axis=-1)  6.87 us
    ppermute x2, waiting for transfers between devices, padded_2(): before = lax.ppermute(last, axis, up)  6.49 us
    concatenate x8, other arithmetic, primitives(): density_all = jnp.concatenate([density] * 4, axis=-1)  6.42 us
    convert_element_type x1, other arithmetic, on_device(): land_weight = jnp.repeat(own_class, tile_columns, total_repeat_length=row...  5.67 us
    gather x2, other arithmetic, on_device(): jnp.repeat(own_class, tile_columns, total_repeat_length=row_total * tile_...  5.58 us
  transfers between devices with their start and end apart: 4, of which 1 were waited for; matrix products, arithmetic and copies ran while one was open for 51% of the time, Pallas kernels for 0%

commit v1 on v0

v1 whole, which is shorter than its diff:
```python
import math

import jax
import jax.numpy as jnp
import numpy as np
from jax import lax
from jax.experimental import pallas as pl
from jax.experimental.pallas import tpu as pltpu
from jax.sharding import PartitionSpec as P

CHUNK = 8
FIRST, SECOND = "first", "second"


def lobatto_derivative():
    points = np.array([-1.0, -math.sqrt(0.2), math.sqrt(0.2), 1.0])
    barycentric = np.array(
        [1.0 / np.prod([points[j] - points[k] for k in range(4) if k != j]) for j in range(4)]
    )
    derivative = np.zeros((4, 4))
    for i in range(4):
        for j in range(4):
            if i != j:
                derivative[i, j] = barycentric[j] / barycentric[i] / (points[i] - points[j])
        derivative[i, i] = -np.sum([derivative[i, k] for k in range(4) if k != i])
    return derivative


def lane_block(shape):
    return lax.broadcasted_iota(jnp.int32, shape, len(shape) - 1) // 32


def spread(values, block, source):
    axis = values.ndim - 1
    if source == 0:
        once = jnp.where(block == 0, values, pltpu.roll(values, 32, axis))
        return jnp.where(block < 2, once, pltpu.roll(once, 64, axis))
    if source == 1:
        once = jnp.where(block == 1, values, pltpu.roll(values, 96, axis))
        return jnp.where(block < 2, once, pltpu.roll(once, 64, axis))
    once = jnp.where(block == 2, values, pltpu.roll(values, 32, axis))
    return jnp.where(block >= 2, once, pltpu.roll(once, 64, axis))


def primitives(states):
    flat = states.reshape(-1, states.shape[-1])
    block = lane_block(flat.shape)
    density = spread(flat, block, 0)
    carried = flat / density
    first = spread(carried, block, 1)
    second = spread(carried, block, 2)
    carried = jnp.where(block == 0, 1.0, carried)
    half_pressure = 0.25 * flat
    zero = jnp.zeros_like(flat)
    pressure_first = jnp.where(block == 1, pltpu.roll(half_pressure, 64, 1), zero)
    pressure_second = jnp.where(block == 2, pltpu.roll(half_pressure, 96, 1), zero)
    back = lambda x: x.reshape(states.shape)
    return {
        "q": states,
        "d": back(density),
        "c": back(carried),
        FIRST: (back(0.125 * first), back(pressure_first)),
        SECOND: (back(0.125 * second), back(pressure_second)),
    }


def pick(prims, index):
    out = {k: prims[k][index] for k in ("q", "d", "c")}
    for k in (FIRST, SECOND):
        out[k] = tuple(x[index] for x in prims[k])
    return out


def flux(one, two, axis):
    return (one["d"] + two["d"]) * (one[axis][0] + two[axis][0]) * (one["c"] + two["c"]) + (
        one[axis][1] + two[axis][1]
    )


def face(left, right, axis):
    wave = 8.0 * jnp.maximum(jnp.abs(left[axis][0]), jnp.abs(right[axis][0])) + 1.0
    return 6.0 * flux(left, right, axis) - (3.0 * wave) * (right["q"] - left["q"])


def volume(nodes, axis):
    derivative = lobatto_derivative()
    fluxes = {}
    for a in range(4):
        for b in range(a + 1, 4):
            fluxes[a, b] = fluxes[b, a] = flux(nodes[a], nodes[b], axis)
    results = []
    for a in range(4):
        total = None
        for b in range(4):
            if b != a:
                term = (-2.0 * float(derivative[a, b])) * fluxes[a, b]
                total = term if total is None else total + term
        results.append(total)
    return results


def silu(z):
    half = 0.5 * z
    return (half + half * jnp.tanh(half)).astype(jnp.bfloat16)


def dot(a, b):
    return jnp.dot(a, b, preferred_element_type=jnp.float32)


def main_kernel(
    air, classes, edge_map, in_w, in_b, mid_w, mid_b, out_w, land_in, land_b, land_out, out, codes
):
    rows, cols, feat = air.shape
    elements = cols // 4
    device_row = lax.axis_index("gx")
    device_col = lax.axis_index("gy")
    for s in range(4):
        codes[s] = edge_map[device_row, s, device_col]

    def chunk(c, carry):
        base_row = pl.multiple_of(c * CHUNK, CHUNK)
        columns = air[pl.ds(base_row, CHUNK)].reshape(CHUNK * cols, feat).astype(jnp.bfloat16)
        values = columns.astype(jnp.float32)
        mean = jnp.sum(values * values, axis=-1, keepdims=True) * (1.0 / feat)
        normed = (values * lax.rsqrt(mean + 1e-06)).astype(jnp.bfloat16)
        hidden = silu(dot(normed, in_w[...]) + in_b[...])
        total = dot(hidden, out_w[...])
        land = silu(dot(normed, land_in[...]) + land_b[...])
        land = silu(dot(land, mid_w[...]) + mid_b[...])
        land_term = dot(land, land_out[...])
        tiles = CHUNK * cols // 64
        pieces = []
        for t in range(tiles):
            weight = classes[device_row, 0, c * tiles + t].astype(jnp.float32)
            cut = slice(t * 64, (t + 1) * 64)
            pieces.append(total[cut] + weight * land_term[cut])
        physics = jnp.concatenate(pieces, axis=0).astype(jnp.bfloat16).astype(jnp.float32)
        out[pl.ds(base_row, CHUNK)] = physics.reshape(CHUNK, cols, feat)

        before = jnp.maximum(base_row - 1, 0)
        after = jnp.minimum(base_row + CHUNK, rows - 1)
        has_before = jnp.where(c > 0, 1.0, 0.0)
        has_after = jnp.where(c < rows // CHUNK - 1, 1.0, 0.0)
        seconds = []
        for a in range(4):
            along = pl.ds(a, elements, stride=4)
            states = air[pl.ds(base_row, CHUNK), along, :]
            prims = primitives(states)
            seconds.append(prims)
            low = primitives(air[pl.ds(before, 1), along, :])
            high = primitives(air[pl.ds(after, 1), along, :])
            result = [None] * CHUNK
            faces = []
            count = CHUNK // 4
            for e in range(count):
                nodes = [pick(prims, slice(e * 4 + k, e * 4 + k + 1)) for k in range(4)]
                if e == 0:
                    faces.append(face(low, nodes[0], FIRST) * has_before)
                else:
                    faces.append(face(last, nodes[0], FIRST))
                last = nodes[3]
                vol = volume(nodes, FIRST)
                for k in range(4):
                    result[e * 4 + k] = vol[k]
            faces.append(face(last, high, FIRST) * has_after)
            for e in range(count):
                result[e * 4] = result[e * 4] + faces[e]
                result[e * 4 + 3] = result[e * 4 + 3] - faces[e + 1]
            for k in range(CHUNK):
                place = (pl.ds(base_row + k, 1), along, slice(None))
                out[place] = out[place] + result[k]
        vol = volume(seconds, SECOND)
        shape = (CHUNK, elements, feat)
        low_nodes = jax.tree.map(lambda x: pltpu.roll(x, 1, 1), seconds[3])
        faces = face(low_nodes, seconds[0], SECOND)
        faces = jnp.where(lax.broadcasted_iota(jnp.int32, shape, 1) == 0, 0.0, faces)
        vol[0] = vol[0] + faces
        vol[3] = vol[3] - pltpu.roll(faces, elements - 1, 1)
        for a in range(4):
            place = (pl.ds(base_row, CHUNK), pl.ds(a, elements, stride=4), slice(None))
            out[place] = out[place] + vol[a]
        return carry

    lax.fori_loop(0, rows // CHUNK, chunk, 0)


def oriented(candidates, code):
    chosen = candidates[code % 4]
    count = chosen.shape[0] // 8
    place = lax.broadcasted_iota(jnp.int32, (8, chosen.shape[1]), 0)
    turned = []
    for k in range(count):
        piece = chosen[(count - 1 - k) * 8 : (count - k) * 8]
        piece = pltpu.roll(piece, 4, 0)
        piece = jnp.where(place % 4 < 2, pltpu.roll(piece, 6, 0), pltpu.roll(piece, 2, 0))
        piece = jnp.where(place % 2 < 1, pltpu.roll(piece, 7, 0), pltpu.roll(piece, 1, 0))
        turned.append(piece)
    return jnp.where(code >= 4, jnp.concatenate(turned, axis=0), chosen)


def edge_kernel(
    codes, edges, west, east, south, north, partial, out, low, high, top, bottom, sems
):
    rows, cols, feat = out.shape
    first, middle, final = pl.ds(0, 8), pl.ds(8, cols - 16), pl.ds(cols - 8, 8)
    places = [
        (low, (slice(None), first)),
        (high, (slice(None), final)),
        (top, (0, middle)),
        (bottom, (rows - 1, middle)),
    ]
    reads = [
        pltpu.make_async_copy(partial.at[p], held, sems.at[k])
        for k, (held, p) in enumerate(places)
    ]
    for copy in reads:
        copy.start()
    own = [primitives(edges[s]) for s in range(4)]
    others = [
        primitives(oriented(ref, codes[s])) for s, ref in enumerate((west, east, south, north))
    ]
    at_west = face(others[0], own[0], FIRST)
    at_east = -face(own[1], others[1], FIRST)
    at_south = face(others[2], own[2], SECOND)
    at_north = -face(own[3], others[3], SECOND)
    for copy in reads:
        copy.wait()
    for held, row, term in ((top, 0, at_west), (bottom, rows - 1, at_east)):
        low[row] = low[row] + term[:8]
        held[...] = held[...] + term[8 : cols - 8]
        high[row] = high[row] + term[cols - 8 :]
    low[:, 0, :] = low[:, 0, :] + at_south
    high[:, 7, :] = high[:, 7, :] + at_north
    writes = [
        pltpu.make_async_copy(held, out.at[p], sems.at[k]) for k, (held, p) in enumerate(places)
    ]
    for copy in writes:
        copy.start()
    for copy in writes:
        copy.wait()


def in_vmem():
    return pl.BlockSpec(memory_space=pltpu.VMEM)


def in_smem():
    return pl.BlockSpec(memory_space=pltpu.SMEM)


def interior(air_state, tile_class, edge_map, weights):
    return pl.pallas_call(
        main_kernel,
        out_shape=[
            jax.ShapeDtypeStruct(air_state.shape, jnp.float32),
            jax.ShapeDtypeStruct((4,), jnp.int32),
        ],
        in_specs=[in_vmem(), in_smem(), in_smem()] + [in_vmem()] * len(weights),
        out_specs=[in_vmem(), in_smem()],
        compiler_params=pltpu.CompilerParams(vmem_limit_bytes=48 * 1024 * 1024),
        cost_estimate=pl.CostEstimate(
            flops=3_200_000_000, bytes_accessed=4_200_000, transcendentals=3_000_000
        ),
        name="columns_and_interior",
    )(air_state, tile_class, edge_map, *weights)


def boundary(codes, edges, traces, partial):
    rows, cols, feat = partial.shape
    return pl.pallas_call(
        edge_kernel,
        out_shape=jax.ShapeDtypeStruct(partial.shape, jnp.float32),
        in_specs=[in_smem()] + [in_vmem()] * 5 + [pl.BlockSpec(memory_space=pl.ANY)],
        out_specs=pl.BlockSpec(memory_space=pl.ANY),
        scratch_shapes=[
            pltpu.VMEM((rows, 8, feat), jnp.float32),
            pltpu.VMEM((rows, 8, feat), jnp.float32),
            pltpu.VMEM((cols - 16, feat), jnp.float32),
            pltpu.VMEM((cols - 16, feat), jnp.float32),
            pltpu.SemaphoreType.DMA((4,)),
        ],
        input_output_aliases={6: 0},
        compiler_params=pltpu.CompilerParams(vmem_limit_bytes=8 * 1024 * 1024),
        cost_estimate=pl.CostEstimate(flops=2_000_000, bytes_accessed=600_000, transcendentals=0),
        name="boundary_faces",
    )(codes, edges, *traces, partial)


def shifted(x, axis, step):
    peers = lax.axis_size(axis)
    return lax.ppermute(x, axis, [(i, (i + step) % peers) for i in range(peers)])


def on_device(
    air_state,
    edge_map,
    tile_class,
    in_weight,
    in_bias,
    mid_weight,
    mid_bias,
    out_weight,
    land_in,
    land_bias,
    land_out,
):
    edges = jnp.stack([air_state[0], air_state[-1], air_state[:, 0], air_state[:, -1]])
    traces = [
        shifted(edges, "gx", 1),
        shifted(edges, "gx", -1),
        shifted(edges, "gy", 1),
        shifted(edges, "gy", -1),
    ]
    weights = (
        in_weight,
        in_bias.reshape(1, -1),
        mid_weight,
        mid_bias.reshape(1, -1),
        out_weight,
        land_in,
        land_bias.reshape(1, -1),
        land_out,
    )
    partial, codes = interior(air_state, tile_class, edge_map.transpose(0, 2, 1), weights)
    return boundary(codes, edges, traces, partial)


def solution(mesh):
    row_split, col_split = P("gx", "gy", None), P(None, "gy", None)
    return jax.shard_map(
        on_device,
        mesh=mesh,
        in_specs=(row_split, P(), col_split) + (P(),) * 8,
        out_specs=row_split,
        check_vma=False,
    )
```

time: 137 us -> 56.9 us (0.42)
  the two profiles are of different devices: /device:TPU:16 before, /device:TPU:15 now
where the time goes in v1:
time: 56.9 us; the launch traced here: 56.2 us
  starting transfers between devices  32.3 us (57%)
  Pallas kernels  12.1 us (21%)
  local copies, waits for them, and re-layouts  11.7 us (21%)
    ppermute x4, starting transfers between devices, shifted(): lax.ppermute(x, axis, [(i, (i + step) % peers) for i in range(peers)])  32.3 us
    unnamed x22, local copies, waits for them, and re-layouts  9.94 us
    pallas_call x1, Pallas kernels, interior(): pl.pallas_call(main_kernel, out_shape=[jax.ShapeDtypeStruct(air_state.sha...  9.6 us
    pallas_call x1, Pallas kernels, boundary(): pl.pallas_call(edge_kernel, out_shape=jax.ShapeDtypeStruct(partial.shape,...  2.47 us
  transfers between devices with their start and end apart: 4, of which 0 were waited for; matrix products, arithmetic and copies ran while one was open for 0% of the time, Pallas kernels for 17%

profile of v1, /device:TPU:15, one launch (start us, length us, event | category | flops | bytes accessed | tf_op | source)
XLA Modules:
  0.0 56.2 jit_solution(3975954447038556143)
XLA Ops:
  0.0 0.7 %fusion = (f32[1,32,128]{2,1,0:T(8,128)S(1)}, f32[1,32,128]{2,1,0:T(8,128)S(1)}) fusion(f32[32,32,128]{2,1,0:T(8,128)} %air.1), kind=kLoop, calls=%fused_computation.1 | loop fusion | bytes 65536 | tf_op jit(solution)/shard_map/slice | solution.py:308
  0.7 1.0 %fusion.1 = (f32[32,1,128]{2,1,0:T(1,128)S(1)}, f32[32,1,128]{2,1,0:T(1,128)S(1)}) fusion(f32[32,32,128]{2,1,0:T(8,128)} %air.1), kind=kLoop, calls=%fused_computation.2 | loop fusion | bytes 65536 | tf_op jit(solution)/shard_map/slice | solution.py:308
  1.8 2.6 %collective-permute-start.3 = (f32[4,32,128]{2,1,0:T(8,128)S(1)}, f32[4,32,128]{2,1,0:T(8,128)S(1)}, u32[]{:S(2)}, u32[]{:S(2)}) collective-permute-start(f32[4,32,128]{2,1,0:T(8,128)S(1)} %pad_maximum_fusion.edges), channel_id=1, source_target_pairs={{0,63},{1,0},{2,1},{3,2},{4,3},{5,4},{6,5},{7,6},{8,7},{9,8},{10,9... | collective-permute-start | bytes 196616 | tf_op jit(solution)/shard_map/ppermute | solution.py:292
  4.3 5.1 %collective-permute-start.2 = (f32[4,32,128]{2,1,0:T(8,128)S(1)}, f32[4,32,128]{2,1,0:T(8,128)S(1)}, u32[]{:S(2)}, u32[]{:S(2)}) collective-permute-start(f32[4,32,128]{2,1,0:T(8,128)S(1)} %pad_maximum_fusion.edges), channel_id=1, source_target_pairs={{0,1},{1,2},{2,3},{3,4},{4,5},{5,6},{6,7},{7,8},{8,9},{9,10},{10,1... | collective-permute-start | bytes 196616 | tf_op jit(solution)/shard_map/ppermute | solution.py:292
  9.4 22.8 %collective-permute-start.1 = (f32[4,32,128]{2,1,0:T(8,128)S(1)}, f32[4,32,128]{2,1,0:T(8,128)S(1)}, u32[]{:S(2)}, u32[]{:S(2)}) collective-permute-start(f32[4,32,128]{2,1,0:T(8,128)S(1)} %pad_maximum_fusion.edges), channel_id=1, source_target_pairs={{0,960},{64,0},{128,64},{192,128},{256,192},{320,256},{384,320},{4... | collective-permute-start | bytes 196616 | tf_op jit(solution)/shard_map/ppermute | solution.py:292
  32.2 1.9 %collective-permute-start = (f32[4,32,128]{2,1,0:T(8,128)S(1)}, f32[4,32,128]{2,1,0:T(8,128)S(1)}, u32[]{:S(2)}, u32[]{:S(2)}) collective-permute-start(f32[4,32,128]{2,1,0:T(8,128)S(1)} %pad_maximum_fusion.edges), channel_id=1, source_target_pairs={{0,64},{64,128},{128,192},{192,256},{256,320},{320,384},{384,448},... | collective-permute-start | bytes 196616 | tf_op jit(solution)/shard_map/ppermute | solution.py:292
  34.1 0.0 copy-start
  34.1 1.0 %copy-done = f32[32,32,128]{2,1,0:T(8,128)S(1)} copy-done((f32[32,32,128]{2,1,0:T(8,128)S(1)}, f32[32,32,128]{2,1,0:T(8,128)}, u32[]{:S(2)}) %copy-start) | copy-done | bytes 524312
  35.2 0.0 copy-start.1
  35.2 1.6 %copy-done.1 = bf16[1024,1024]{1,0:T(8,128)(2,1)S(1)} copy-done((bf16[1024,1024]{1,0:T(8,128)(2,1)S(1)}, bf16[1024,1024]{1,0:T(8,128)(2,1)}, u32[]{:S(2)}) %copy-start.1) | copy-done | bytes 2097176
  36.8 0.0 copy-start.2
  36.8 0.9 %copy-done.2 = bf16[128,1024]{1,0:T(8,128)(2,1)S(1)} copy-done((bf16[128,1024]{1,0:T(8,128)(2,1)S(1)}, bf16[128,1024]{1,0:T(8,128)(2,1)}, u32[]{:S(2)}) %copy-start.2) | copy-done | bytes 262168
  37.7 0.0 copy-start.3
  37.7 0.9 %copy-done.3 = bf16[1024,128]{1,0:T(8,128)(2,1)S(1)} copy-done((bf16[1024,128]{1,0:T(8,128)(2,1)S(1)}, bf16[1024,128]{1,0:T(8,128)(2,1)}, u32[]{:S(2)}) %copy-start.3) | copy-done | bytes 262168
  38.7 0.9 %copy-done.4 = bf16[128,1024]{1,0:T(8,128)(2,1)S(1)} copy-done((bf16[128,1024]{1,0:T(8,128)(2,1)S(1)}, bf16[128,1024]{1,0:T(8,128)(2,1)}, u32[]{:S(2)}) %copy-start.4) | copy-done | bytes 262168
  39.6 0.0 copy-start.5
  39.6 0.9 %copy-done.5 = bf16[1024,128]{1,0:T(8,128)(2,1)S(1)} copy-done((bf16[1024,128]{1,0:T(8,128)(2,1)S(1)}, bf16[1024,128]{1,0:T(8,128)(2,1)}, u32[]{:S(2)}) %copy-start.5) | copy-done | bytes 262168
  40.6 0.0 copy-start.6
  40.6 0.8 %copy-done.6 = s32[16,64,4]{1,2,0:T(4,128)S(1)} copy-done((s32[16,64,4]{1,2,0:T(4,128)S(1)}, s32[16,64,4]{1,2,0:T(4,128)}, u32[]{:S(2)}) %copy-start.6) | copy-done | bytes 16408
  41.3 0.0 copy-start.7
  41.3 0.7 %copy-done.7 = s32[16,1,16]{2,1,0:T(1,128)S(1)} copy-done((s32[16,1,16]{2,1,0:T(1,128)S(1)}, s32[16,1,16]{2,1,0:T(1,128)}, u32[]{:S(2)}) %copy-start.7) | copy-done | bytes 1048
  42.0 0.0 copy-start.8
  42.0 0.7 %copy-done.8 = f32[1024]{0:T(1024)S(1)} copy-done((f32[1024]{0:T(1024)S(1)}, f32[1024]{0:T(1024)}, u32[]{:S(2)}) %copy-start.8) | copy-done | bytes 4120
  42.7 0.0 copy-start.9
  42.7 0.7 %copy-done.9 = f32[1024]{0:T(1024)S(1)} copy-done((f32[1024]{0:T(1024)S(1)}, f32[1024]{0:T(1024)}, u32[]{:S(2)}) %copy-start.9) | copy-done | bytes 4120
  43.4 0.7 %copy-done.10 = f32[1024]{0:T(1024)S(1)} copy-done((f32[1024]{0:T(1024)S(1)}, f32[1024]{0:T(1024)}, u32[]{:S(2)}) %copy-start.10) | copy-done | bytes 4120
  44.1 9.6 %columns_and_interior.1 = (f32[32,32,128]{2,1,0:T(8,128)}, s32[4]{0:T(128)S(1)}) custom-call(f32[32,32,128]{2,1,0:T(8,128)S(1)} %copy-done, s32[16,1,16]{2,1,0:T(1,128)S(1)} %copy-done.7, s32[16,4,64]{2,1,0:T(4,128)S(1)} %bitcast.10, bf16[128,1024]{1,0:T(8,128)(2,1)S(1)} %copy-done.2, f32[1,1024]{1,0:T(1,128)S(1)} %bitcast.11, ...), custom_call_target="tpu_custom_call" | custom-call | flops 3200000000 | bytes 4200000 | tf_op jit(solution)/shard_map/columns_and_interior/pallas_call | solution.py:253
  53.7 0.0 collective-permute-done.3.north
  53.7 0.0 collective-permute-done.2.south
  53.7 0.0 collective-permute-done.1.east
  53.7 0.0 collective-permute-done.west
  53.7 2.5 %boundary_faces.1 = f32[32,32,128]{2,1,0:T(8,128)} custom-call(s32[4]{0:T(128)S(1)} %get-tuple-element.7.codes, f32[4,32,128]{2,1,0:T(8,128)S(1)} %pad_maximum_fusion.edges, f32[4,32,128]{2,1,0:T(8,128)S(1)} %collective-permute-done.west, f32[4,32,128]{2,1,0:T(8,128)S(1)} %collective-permute-done.1.east, ...), custom_call_target="tpu_custom_call", output_to_operand_aliasing={{}: (6, {})} | custom-call | flops 2000000 | bytes 600000 | tf_op jit(solution)/shard_map/boundary_faces/pallas_call | solution.py:271
  (3 shorter events, 0.0 us)
Async XLA Ops:
  1.8 51.9 %collective-permute-start.3 = (f32[4,32,128]{2,1,0:T(8,128)S(1)}, f32[4,32,128]{2,1,0:T(8,128)S(1)}, u32[]{:S(2)}, u32[]{:S(2)}) collective-permute-start(f32[4,32,128]{2,1,0:T(8,128)S(1)} %pad_maximum_fusion.edges), channel_id=1, source_target_pairs={{0,63},{1,0},{2,1},{3,2},{4,3},{5,4},{6,5},{7,6},{8,7},{9,8},{10,9... | collective-permute-start | bytes 196616 | tf_op jit(solution)/shard_map/ppermute | solution.py:292
  4.3 49.4 %collective-permute-start.2 = (f32[4,32,128]{2,1,0:T(8,128)S(1)}, f32[4,32,128]{2,1,0:T(8,128)S(1)}, u32[]{:S(2)}, u32[]{:S(2)}) collective-permute-start(f32[4,32,128]{2,1,0:T(8,128)S(1)} %pad_maximum_fusion.edges), channel_id=1, source_target_pairs={{0,1},{1,2},{2,3},{3,4},{4,5},{5,6},{6,7},{7,8},{8,9},{9,10},{10,1... | collective-permute-start | bytes 196616 | tf_op jit(solution)/shard_map/ppermute | solution.py:292
  9.4 44.3 %collective-permute-start.1 = (f32[4,32,128]{2,1,0:T(8,128)S(1)}, f32[4,32,128]{2,1,0:T(8,128)S(1)}, u32[]{:S(2)}, u32[]{:S(2)}) collective-permute-start(f32[4,32,128]{2,1,0:T(8,128)S(1)} %pad_maximum_fusion.edges), channel_id=1, source_target_pairs={{0,960},{64,0},{128,64},{192,128},{256,192},{320,256},{384,320},{4... | collective-permute-start | bytes 196616 | tf_op jit(solution)/shard_map/ppermute | solution.py:292
  32.2 21.5 %collective-permute-start = (f32[4,32,128]{2,1,0:T(8,128)S(1)}, f32[4,32,128]{2,1,0:T(8,128)S(1)}, u32[]{:S(2)}, u32[]{:S(2)}) collective-permute-start(f32[4,32,128]{2,1,0:T(8,128)S(1)} %pad_maximum_fusion.edges), channel_id=1, source_target_pairs={{0,64},{64,128},{128,192},{192,256},{256,320},{320,384},{384,448},... | collective-permute-start | bytes 196616 | tf_op jit(solution)/shard_map/ppermute | solution.py:292
  34.1 1.0 %copy-start = (f32[32,32,128]{2,1,0:T(8,128)S(1)}, f32[32,32,128]{2,1,0:T(8,128)}, u32[]{:S(2)}) copy-start(f32[32,32,128]{2,1,0:T(8,128)} %air.1) | copy-start | bytes 1572868
  35.2 1.6 %copy-start.1 = (bf16[1024,1024]{1,0:T(8,128)(2,1)S(1)}, bf16[1024,1024]{1,0:T(8,128)(2,1)}, u32[]{:S(2)}) copy-start(bf16[1024,1024]{1,0:T(8,128)(2,1)} %mid_w.1) | copy-start | bytes 6291460
  36.8 0.9 %copy-start.2 = (bf16[128,1024]{1,0:T(8,128)(2,1)S(1)}, bf16[128,1024]{1,0:T(8,128)(2,1)}, u32[]{:S(2)}) copy-start(bf16[128,1024]{1,0:T(8,128)(2,1)} %in_w.1) | copy-start | bytes 786436
  37.7 0.9 %copy-start.3 = (bf16[1024,128]{1,0:T(8,128)(2,1)S(1)}, bf16[1024,128]{1,0:T(8,128)(2,1)}, u32[]{:S(2)}) copy-start(bf16[1024,128]{1,0:T(8,128)(2,1)} %out_w.1) | copy-start | bytes 786436
  38.7 0.9 %copy-start.4 = (bf16[128,1024]{1,0:T(8,128)(2,1)S(1)}, bf16[128,1024]{1,0:T(8,128)(2,1)}, u32[]{:S(2)}) copy-start(bf16[128,1024]{1,0:T(8,128)(2,1)} %land_in.1) | copy-start | bytes 786436
  39.6 0.9 %copy-start.5 = (bf16[1024,128]{1,0:T(8,128)(2,1)S(1)}, bf16[1024,128]{1,0:T(8,128)(2,1)}, u32[]{:S(2)}) copy-start(bf16[1024,128]{1,0:T(8,128)(2,1)} %land_out.1) | copy-start | bytes 786436
  40.6 0.8 %copy-start.6 = (s32[16,64,4]{1,2,0:T(4,128)S(1)}, s32[16,64,4]{1,2,0:T(4,128)}, u32[]{:S(2)}) copy-start(s32[16,64,4]{1,2,0:T(4,128)} %param.12) | copy-start | bytes 49156
  41.3 0.7 %copy-start.7 = (s32[16,1,16]{2,1,0:T(1,128)S(1)}, s32[16,1,16]{2,1,0:T(1,128)}, u32[]{:S(2)}) copy-start(s32[16,1,16]{2,1,0:T(1,128)} %classes.1) | copy-start | bytes 3076
  42.0 0.7 %copy-start.8 = (f32[1024]{0:T(1024)S(1)}, f32[1024]{0:T(1024)}, u32[]{:S(2)}) copy-start(f32[1024]{0:T(1024)} %param.15) | copy-start | bytes 12292
  42.7 0.7 %copy-start.9 = (f32[1024]{0:T(1024)S(1)}, f32[1024]{0:T(1024)}, u32[]{:S(2)}) copy-start(f32[1024]{0:T(1024)} %param.17) | copy-start | bytes 12292
  43.4 0.7 %copy-start.10 = (f32[1024]{0:T(1024)S(1)}, f32[1024]{0:T(1024)}, u32[]{:S(2)}) copy-start(f32[1024]{0:T(1024)} %param.20) | copy-start | bytes 12292

commit v2 on v1

v2 whole, which is shorter than its diff:
```python
import functools
import math

import jax
import jax.numpy as jnp
import numpy as np
from jax import lax
from jax.experimental import pallas as pl
from jax.experimental.pallas import tpu as pltpu
from jax.sharding import PartitionSpec as P

CHUNK = 16
TILE = 64
GROUP = 8
WRAP = 8
FIRST, SECOND = "first", "second"


def lobatto_derivative():
    points = np.array([-1.0, -math.sqrt(0.2), math.sqrt(0.2), 1.0])
    barycentric = np.array(
        [1.0 / np.prod([points[j] - points[k] for k in range(4) if k != j]) for j in range(4)]
    )
    derivative = np.zeros((4, 4))
    for i in range(4):
        for j in range(4):
            if i != j:
                derivative[i, j] = barycentric[j] / barycentric[i] / (points[i] - points[j])
        derivative[i, i] = -np.sum([derivative[i, k] for k in range(4) if k != i])
    return derivative


def lane_block(shape):
    return lax.broadcasted_iota(jnp.int32, shape, len(shape) - 1) // 32


def spread(values, block, source):
    axis = values.ndim - 1
    if source == 0:
        once = jnp.where(block == 0, values, pltpu.roll(values, 32, axis))
        return jnp.where(block < 2, once, pltpu.roll(once, 64, axis))
    if source == 1:
        once = jnp.where(block == 1, values, pltpu.roll(values, 96, axis))
        return jnp.where(block < 2, once, pltpu.roll(once, 64, axis))
    once = jnp.where(block == 2, values, pltpu.roll(values, 32, axis))
    return jnp.where(block >= 2, once, pltpu.roll(once, 64, axis))


def primitives(states):
    flat = states.reshape(-1, states.shape[-1])
    block = lane_block(flat.shape)
    density = spread(flat, block, 0)
    carried = flat / density
    first = spread(carried, block, 1)
    second = spread(carried, block, 2)
    carried = jnp.where(block == 0, 1.0, carried)
    half_pressure = 0.25 * flat
    zero = jnp.zeros_like(flat)
    pressure_first = jnp.where(block == 1, pltpu.roll(half_pressure, 64, 1), zero)
    pressure_second = jnp.where(block == 2, pltpu.roll(half_pressure, 96, 1), zero)
    back = lambda x: x.reshape(states.shape)
    return {
        "q": states,
        "d": back(density),
        "c": back(carried),
        FIRST: (back(0.125 * first), back(pressure_first)),
        SECOND: (back(0.125 * second), back(pressure_second)),
    }


def pick(prims, index):
    out = {k: prims[k][index] for k in ("q", "d", "c")}
    for k in (FIRST, SECOND):
        out[k] = tuple(x[index] for x in prims[k])
    return out


def flux(one, two, axis):
    return (one["d"] + two["d"]) * (one[axis][0] + two[axis][0]) * (one["c"] + two["c"]) + (
        one[axis][1] + two[axis][1]
    )


def face(left, right, axis):
    wave = 8.0 * jnp.maximum(jnp.abs(left[axis][0]), jnp.abs(right[axis][0])) + 1.0
    return 6.0 * flux(left, right, axis) - (3.0 * wave) * (right["q"] - left["q"])


def volume(nodes, axis):
    derivative = lobatto_derivative()
    fluxes = {}
    for a in range(4):
        for b in range(a + 1, 4):
            fluxes[a, b] = fluxes[b, a] = flux(nodes[a], nodes[b], axis)
    results = []
    for a in range(4):
        total = None
        for b in range(4):
            if b != a:
                term = (-2.0 * float(derivative[a, b])) * fluxes[a, b]
                total = term if total is None else total + term
        results.append(total)
    return results


def silu(z):
    half = 0.5 * z
    return (half + half * jnp.tanh(half)).astype(jnp.bfloat16)


def dot(a, b):
    return jnp.dot(a, b, preferred_element_type=jnp.float32)


def ahead(row, col):
    return (row % WRAP == 0) & ((row > 0) | (col > 0))


def turned(edge):
    count = edge.shape[0] // 8
    place = lax.broadcasted_iota(jnp.int32, (8, edge.shape[1]), 0)
    pieces = []
    for k in range(count):
        piece = edge[(count - 1 - k) * 8 : (count - k) * 8]
        piece = pltpu.roll(piece, 4, 0)
        piece = jnp.where(place % 4 < 2, pltpu.roll(piece, 6, 0), pltpu.roll(piece, 2, 0))
        piece = jnp.where(place % 2 < 1, pltpu.roll(piece, 7, 0), pltpu.roll(piece, 1, 0))
        pieces.append(piece)
    return jnp.concatenate(pieces, axis=0)


def pack_kernel(n_x, n_y, air, edge_map, own, wrap, row_even, row_odd, col_even, col_odd, back, maps, sems):
    rows, cols, _ = air.shape
    row, col = lax.axis_index("gx"), lax.axis_index("gy")
    west, east = (row + n_x - 1) % n_x, (row + 1) % n_x
    south, north = (col + n_y - 1) % n_y, (col + 1) % n_y
    copies = [
        pltpu.make_async_copy(air.at[:, 0], own.at[2], sems.at[0]),
        pltpu.make_async_copy(air.at[:, cols - 1], own.at[3], sems.at[1]),
        pltpu.make_async_copy(air.at[0], own.at[0], sems.at[2]),
        pltpu.make_async_copy(air.at[rows - 1], own.at[1], sems.at[3]),
        pltpu.make_async_copy(edge_map.at[west], maps.at[0], sems.at[4]),
        pltpu.make_async_copy(edge_map.at[row], maps.at[1], sems.at[5]),
        pltpu.make_async_copy(edge_map.at[east], maps.at[2], sems.at[6]),
    ]
    for copy in copies:
        copy.start()
    for copy in copies:
        copy.wait()

    def asked(code):
        edge = own[code % 4]
        return jnp.where(code >= 4, turned(edge), edge)

    to_west = asked(maps[0, 1, col])
    to_east = asked(maps[2, 0, col])
    to_south = asked(maps[1, 3, south])
    to_north = asked(maps[1, 2, north])
    even = row % 2 == 0
    row_even[...] = jnp.where(even, to_east, to_west)
    odd = jnp.where(even, to_west, to_east)
    row_odd[...] = odd
    wrap[...] = odd
    back[...] = odd
    even = col % 2 == 0
    col_even[...] = jnp.where(even, to_north, to_south)
    col_odd[...] = jnp.where(even, to_south, to_north)


def main_kernel(early, inputs, moved, result, scratch):
    held, sems, move_sems, normed, base, listed, fields, total = scratch
    row = lax.axis_index("gx")
    col = lax.axis_index("gy")
    moves = start_moves(moved, move_sems, row)

    @pl.when(ahead(row, col) == early)
    def _():
        copies = []
        for k, (source, target) in enumerate(zip(inputs, held)):
            if k == 1:
                source = source.at[row]
            copies.append(pltpu.make_async_copy(source, target, sems.at[k]))
        for k in (0, 2, 3, 6, 1, 7, 8, 4, 5, 9):
            copies[k].start()

        def ready(*numbers):
            for k in numbers:
                copies[k].wait()

        columns_and_interior(held, ready, normed, base, listed, fields, total)
        end = pltpu.make_async_copy(total, result, sems.at[0])
        end.start()
        end.wait()

    end_moves(moves, row)


def start_moves(moved, sems, row):
    moves = []
    for sources, target, wanted in moved:
        first = sum(len(copies) for copies, _ in moves)
        copies = [
            pltpu.make_async_copy(ref, target.at[k], sems.at[first + k])
            for k, ref in enumerate(sources)
        ]
        moves.append((copies, wanted))
    for copies, wanted in moves:

        @pl.when(wanted(row))
        def _():
            for copy in copies:
                copy.start()

    return moves


def end_moves(moves, row):
    for copies, wanted in moves:

        @pl.when(wanted(row))
        def _():
            for copy in copies:
                copy.wait()


def two_layers(x, weight, bias, last):
    return dot(silu(dot(x, weight[...]) + bias[...]), last[...])


def columns_and_interior(held, ready, normed_ref, base, listed, fields, out):
    air, classes, in_w, in_b, mid_w, mid_b, out_w, land_in, land_b, land_out = held
    rows, cols, feat = air.shape
    tiles = rows * cols // TILE
    chunk_cols = CHUNK * cols

    ready(0, 2, 3, 6)

    def base_chunk(c, carry):
        start = pl.multiple_of(c * CHUNK, CHUNK)
        columns = air[pl.ds(start, CHUNK)].reshape(chunk_cols, feat).astype(jnp.bfloat16)
        values = columns.astype(jnp.float32)
        mean = jnp.sum(values * values, axis=-1, keepdims=True) * (1.0 / feat)
        normed = (values * lax.rsqrt(mean + 1e-06)).astype(jnp.bfloat16)
        place = pl.ds(pl.multiple_of(c * chunk_cols, chunk_cols), chunk_cols)
        normed_ref[place, :] = normed
        base[place, :] = two_layers(normed, in_w, in_b, out_w)
        store_fields(start, CHUNK, air, fields)
        return carry

    lax.fori_loop(0, rows // CHUNK, base_chunk, 0)

    ready(1)

    def note(t, count):
        listed[count] = t
        return count + classes[0, t]

    lands = lax.fori_loop(0, tiles, note, 0)
    for k in range(GROUP):
        listed[lands + k] = tiles

    @pl.when(lands > 0)
    def _():
        ready(4, 5, 7, 8, 9)

    def land_group(g, carry):
        numbers = [listed[g * GROUP + k] for k in range(GROUP)]
        starts = [pl.multiple_of(t * TILE, TILE) for t in numbers]
        normed = jnp.concatenate([normed_ref[pl.ds(s, TILE), :] for s in starts], axis=0)
        land = silu(dot(normed, land_in[...]) + land_b[...])
        term = two_layers(land, mid_w, mid_b, land_out)
        for k, s in enumerate(starts):
            base[pl.ds(s, TILE), :] = base[pl.ds(s, TILE), :] + term[k * TILE : (k + 1) * TILE]
        return carry

    lax.fori_loop(0, (lands + GROUP - 1) // GROUP, land_group, 0)
    interior_and_sum(air, fields, base, out)

    @pl.when(lands == 0)
    def _():
        ready(4, 5, 7, 8, 9)


def store_fields(start, count, air, fields):
    _, cols, feat = air.shape
    elements = cols // 4
    for a in range(4):
        states = air[pl.ds(start, count), pl.ds(a, elements, stride=4), :]
        flat = states.reshape(-1, feat)
        block = lane_block(flat.shape)
        density = spread(flat, block, 0)
        carried = flat * pl.reciprocal(density)
        speeds = 0.125 * carried
        half_pressure = 0.25 * flat
        values = (
            density,
            jnp.where(block == 0, 1.0, carried),
            spread(speeds, block, 1),
            spread(speeds, block, 2),
            jnp.where(block == 1, pltpu.roll(half_pressure, 64, 1), 0.0),
            jnp.where(block == 2, pltpu.roll(half_pressure, 96, 1), 0.0),
        )
        for k, value in enumerate(values):
            fields[k, pl.ds(start, count), a] = value.reshape(states.shape)


def node_fields(fields, row, a):
    d, c, u, v, p, s = (fields[k, row, a] for k in range(6))
    return {"d": d, "c": c, "q": d * c, FIRST: (u, p), SECOND: (v, s)}


def interior_and_sum(air, fields, base, out):
    rows, cols, feat = air.shape
    elements = cols // 4
    count = rows // 4
    number = lax.broadcasted_iota(jnp.int32, (elements, feat), 0)

    def element(e, below):
        start = e * 4
        after = jnp.minimum(start + 4, rows - 1)
        inside = jnp.where(e < count - 1, 1.0, 0.0)
        sums = [[None] * 4 for _ in range(4)]
        above = []
        for a in range(4):
            nodes = [node_fields(fields, start + r, a) for r in range(4)]
            totals = volume(nodes, FIRST)
            high = inside * face(nodes[3], node_fields(fields, after, a), FIRST)
            above.append(high)
            totals[0] = totals[0] + below[a]
            totals[3] = totals[3] - high
            for r in range(4):
                sums[r][a] = totals[r]
        for r in range(4):
            nodes = [node_fields(fields, start + r, a) for a in range(4)]
            totals = volume(nodes, SECOND)
            lower = jax.tree.map(lambda x: pltpu.roll(x, 1, 0), nodes[3])
            faces = jnp.where(number == 0, 0.0, face(lower, nodes[0], SECOND))
            totals[0] = totals[0] + faces
            totals[3] = totals[3] - pltpu.roll(faces, elements - 1, 0)
            for a in range(4):
                along = pl.ds(a, elements, stride=4)
                out[start + r, along, :] = sums[r][a] + totals[a]
        physics = base[pl.ds(pl.multiple_of(start * cols, 4 * cols), 4 * cols), :]
        physics = physics.astype(jnp.bfloat16).astype(jnp.float32).reshape(4, cols, feat)
        out[pl.ds(start, 4)] = out[pl.ds(start, 4)] + physics
        return tuple(above)

    zero = jnp.zeros((elements, feat), jnp.float32)
    lax.fori_loop(0, count, element, (zero,) * 4)


def edge_kernel(edges, early, late, from_low, from_high, partial, out, low, high, top, bottom, sems):
    col_even_a, col_odd_a, row_odd_a, row_even_a = (early[k] for k in range(4))
    col_even_b, col_odd_b, row_even_b = (late[k] for k in range(3))
    rows, cols, feat = out.shape
    first, middle, final = pl.ds(0, 8), pl.ds(8, cols - 16), pl.ds(cols - 8, 8)
    inner = (pl.ds(1, rows - 2), middle)
    inside = pltpu.make_async_copy(partial.at[inner], out.at[inner], sems.at[4])
    inside.start()
    row, col = lax.axis_index("gx"), lax.axis_index("gy")
    place = row % WRAP
    last_row = place == WRAP - 1
    first_x = jnp.where(place < WRAP - 2, row_even_a, row_even_b)
    wrapped = jnp.where(place == 0, from_low[...], from_high[...])
    second_x = jnp.where((place == 0) | last_row, wrapped, row_odd_a)
    even = row % 2 == 0
    west = jnp.where(even, second_x, first_x)
    east = jnp.where(even, first_x, second_x)
    first_y = jnp.where(last_row, col_even_b, col_even_a)
    second_y = jnp.where(last_row, col_odd_b, col_odd_a)
    even = col % 2 == 0
    south = jnp.where(even, second_y, first_y)
    north = jnp.where(even, first_y, second_y)
    own = [primitives(edges[s]) for s in range(4)]
    west, east, south, north = (primitives(x) for x in (west, east, south, north))
    at_west = face(west, own[0], FIRST)
    at_east = -face(own[1], east, FIRST)
    at_south = face(south, own[2], SECOND)
    at_north = -face(own[3], north, SECOND)
    low[...] = partial[:, :8]
    high[...] = partial[:, cols - 8 :]
    for held, r, term in ((top, 0, at_west), (bottom, rows - 1, at_east)):
        low[r] = low[r] + term[:8]
        held[...] = partial[r, 8 : cols - 8] + term[8 : cols - 8]
        high[r] = high[r] + term[cols - 8 :]
    low[:, 0, :] = low[:, 0, :] + at_south
    high[:, 7, :] = high[:, 7, :] + at_north
    places = [
        (low, (slice(None), first)),
        (high, (slice(None), final)),
        (top, (0, middle)),
        (bottom, (rows - 1, middle)),
    ]
    writes = [
        pltpu.make_async_copy(held, out.at[p], sems.at[k]) for k, (held, p) in enumerate(places)
    ]
    for copy in writes:
        copy.start()
    for copy in writes:
        copy.wait()
    inside.wait()


def in_vmem():
    return pl.BlockSpec(memory_space=pltpu.VMEM)


def in_hbm():
    return pl.BlockSpec(memory_space=pltpu.HBM)


def anywhere():
    return pl.BlockSpec(memory_space=pl.ANY)


def kept_in_hbm(x):
    return pltpu.with_memory_space_constraint(x, pltpu.HBM)


def vmem_array(shape, dtype):
    return pltpu.VMEM(shape, dtype)


def kept_in_vmem(x):
    return pltpu.with_memory_space_constraint(x, pltpu.VMEM)


def packed(air_state, edge_map, n_x, n_y):
    rows, cols, feat = air_state.shape
    return pl.pallas_call(
        functools.partial(pack_kernel, n_x, n_y),
        out_shape=[vmem_array((4, cols, feat), jnp.float32)]
        + [vmem_array((cols, feat), jnp.float32)] * 6,
        in_specs=[in_hbm()] * 2,
        out_specs=[in_vmem()] * 7,
        scratch_shapes=[
            pltpu.SMEM((3,) + edge_map.shape[1:], jnp.int32),
            pltpu.SemaphoreType.DMA((7,)),
        ],
        compiler_params=pltpu.CompilerParams(vmem_limit_bytes=4 * 1024 * 1024),
        name="own_edges",
    )(kept_in_hbm(air_state), kept_in_hbm(edge_map))


def idle_kernel(*refs):
    pass


def nothing(count):
    def make(*edges):
        x = edges[0]
        return tuple(
            pl.pallas_call(
                idle_kernel,
                out_shape=[jax.ShapeDtypeStruct(x.shape, x.dtype)] * count,
                in_specs=[anywhere()],
                out_specs=[anywhere()] * count,
                name="no_exchange",
            )(x)
        )

    return make


def interior(early, inputs, passed, started=(), groups=()):
    air_state = inputs[0]
    held = []
    for k, x in enumerate(inputs):
        space = pltpu.SMEM if k == 1 else pltpu.VMEM
        held.append(space(x.shape[1:] if k == 1 else x.shape, x.dtype))
    like = lambda x: vmem_array(x.shape, x.dtype)
    outs = [vmem_array(air_state.shape, jnp.float32)]
    outs += [like(x) for x in started[1:]]
    n_in, n_passed, n_started = len(inputs), len(passed), len(started)
    targets = []
    for arrays, _, number in groups:
        targets.append(len(outs) if number is None else number)
        if number is None:
            outs.append(vmem_array((len(arrays),) + arrays[0].shape, arrays[0].dtype))
    every = [x for arrays, _, _ in groups for x in arrays]
    n_fixed = len(outs)
    aliases = {n_in + k: n_fixed + k for k in range(n_passed)}
    aliases.update({n_in + n_passed + k: k for k in range(n_started)})
    rows, cols, feat = air_state.shape
    tiles = rows * cols // TILE

    def kernel(*refs):
        refs = list(refs)
        n_before = n_in + n_passed + n_started
        results = refs[n_before + len(every) :][: n_fixed + n_passed]
        rest = refs[n_before + len(every) + len(results) :]
        moved, at = [], n_before
        for (arrays, wanted, _), target in zip(groups, targets):
            moved.append((refs[at : at + len(arrays)], results[target], wanted))
            at += len(arrays)
        main_kernel(early, refs[:n_in], moved, results[0], (rest[:n_in], *rest[n_in:]))

    return pl.pallas_call(
        kernel,
        out_shape=outs + [like(x) for x in passed],
        in_specs=[in_hbm()] * n_in
        + [in_vmem()] * (n_passed + n_started)
        + [anywhere()] * len(every),
        out_specs=[in_vmem()] * (n_fixed + n_passed),
        scratch_shapes=held
        + [
            pltpu.SemaphoreType.DMA((n_in,)),
            pltpu.SemaphoreType.DMA((max(len(every), 1),)),
            pltpu.VMEM((rows * cols + TILE, feat), jnp.bfloat16),
            pltpu.VMEM((rows * cols + TILE, feat), jnp.float32),
            pltpu.SMEM((tiles + GROUP,), jnp.int32),
            pltpu.VMEM((6, rows, 4, cols // 4, feat), jnp.float32),
            pltpu.VMEM(air_state.shape, jnp.float32),
        ],
        input_output_aliases=aliases,
        compiler_params=pltpu.CompilerParams(vmem_limit_bytes=32 * 1024 * 1024),
        cost_estimate=pl.CostEstimate(
            flops=1_000_000_000, bytes_accessed=4_200_000, transcendentals=1_000_000
        ),
        name="columns_ahead" if early else "columns_behind",
    )(*map(kept_in_hbm, inputs), *map(kept_in_vmem, (*passed, *started)), *every)


def collected(arrays, wanted, passed):
    count, n_passed = len(arrays), len(passed)
    like = lambda x: vmem_array(x.shape, x.dtype)

    def kernel(*refs):
        row = lax.axis_index("gx")
        sources, target, sems = refs[:count], refs[count + n_passed], refs[-1]
        end_moves(start_moves([(sources, target, wanted)], sems, row), row)

    return pl.pallas_call(
        kernel,
        out_shape=[vmem_array((count,) + arrays[0].shape, arrays[0].dtype)]
        + [like(x) for x in passed],
        in_specs=[anywhere()] * count + [in_vmem()] * n_passed,
        out_specs=[in_vmem()] * (1 + n_passed),
        scratch_shapes=[pltpu.SemaphoreType.DMA((count,))],
        input_output_aliases={count + k: 1 + k for k in range(n_passed)},
        name="early_traces",
    )(*arrays, *map(kept_in_vmem, passed))


def boundary(edges, early, late, from_low, from_high, partial):
    rows, cols, feat = partial.shape
    return pl.pallas_call(
        edge_kernel,
        out_shape=jax.ShapeDtypeStruct(partial.shape, jnp.float32),
        in_specs=[in_vmem()] * 6,
        out_specs=in_hbm(),
        scratch_shapes=[
            pltpu.VMEM((rows, 8, feat), jnp.float32),
            pltpu.VMEM((rows, 8, feat), jnp.float32),
            pltpu.VMEM((cols - 16, feat), jnp.float32),
            pltpu.VMEM((cols - 16, feat), jnp.float32),
            pltpu.SemaphoreType.DMA((5,)),
        ],
        compiler_params=pltpu.CompilerParams(vmem_limit_bytes=8 * 1024 * 1024),
        cost_estimate=pl.CostEstimate(flops=2_000_000, bytes_accessed=600_000, transcendentals=0),
        name="boundary_faces",
    )(edges, early, late, from_low, from_high, partial)


def swap(rows, cols, n_y):
    pairs = []
    for r, other_r in rows:
        for c, other_c in cols:
            one, two = r * n_y + c, other_r * n_y + other_c
            pairs += [(one, two), (two, one)]
    return pairs


def on_device(
    air_state,
    edge_map,
    tile_class,
    in_weight,
    in_bias,
    mid_weight,
    mid_bias,
    out_weight,
    land_in,
    land_bias,
    land_out,
):
    n_x, n_y = lax.axis_size("gx"), lax.axis_size("gy")
    inputs = (
        air_state,
        tile_class,
        in_weight,
        in_bias.reshape(1, -1),
        mid_weight,
        mid_bias.reshape(1, -1),
        out_weight,
        land_in,
        land_bias.reshape(1, -1),
        land_out,
    )
    row = lax.axis_index("gx")
    late = [i for i in range(n_x) if i % WRAP == WRAP - 1]
    early = [i for i in range(n_x) if i not in late]
    evens = [(i, i + 1) for i in range(0, n_x, 2)]
    odds = [(i, (i + 1) % n_x) for i in range(1, n_x, 2)]
    col_evens = [(j, j + 1) for j in range(0, n_y, 2)]
    col_odds = [(j, (j + 1) % n_y) for j in range(1, n_y, 2)]
    col_same = [(j, j) for j in range(n_y)]

    def move(x, rows, cols):
        return lax.ppermute(x, ("gx", "gy"), swap(rows, cols, n_y))

    def exchange_early(row_even, row_odd, col_odd, col_even):
        same = [(i, i) for i in early]
        return (
            move(col_even, same, col_evens),
            move(col_odd, same, col_odds),
            move(row_odd, [p for p in odds if p[0] not in late], col_same),
            move(row_even, [p for p in evens if p[1] not in late], col_same),
        )

    def exchange_late(row_even, col_odd, col_even):
        same = [(i, i) for i in late]
        return (
            move(col_even, same, col_evens),
            move(col_odd, same, col_odds),
            move(row_even, [p for p in evens if p[1] in late], col_same),
        )

    def across(x, rows):
        return lax.ppermute(
            x, ("gx", "gy"), [(a * n_y + j, b * n_y + j) for a, b in rows for j in range(n_y)]
        )

    place = row % WRAP
    wraps = [p for p in odds if p[0] in late]
    is_first = lambda r: r % WRAP == 0
    is_middle = lambda r: (r % WRAP > 0) & (r % WRAP < WRAP - 1)
    is_late = lambda r: r % WRAP >= WRAP - 2
    own, wrap, row_even, row_odd, col_even, col_odd, back = packed(
        air_state, edge_map.transpose(0, 2, 1), n_x, n_y
    )
    partial, wrap, row_even, row_odd, col_even, col_odd, back = interior(
        True, inputs, (wrap, row_even, row_odd, col_even, col_odd, back)
    )
    from_low = across(wrap, wraps)
    early_traces = lax.cond(
        place < WRAP - 1, exchange_early, nothing(4), row_even, row_odd, col_odd, col_even
    )
    early_held, back = collected(early_traces, is_first, (back,))
    from_high = across(back, [(b, a) for a, b in wraps])
    late_traces = lax.cond(
        place >= WRAP - 2, exchange_late, nothing(3), row_even, col_odd, col_even
    )
    partial, early_held, late_held = interior(
        False,
        inputs,
        (),
        (partial, early_held),
        ((early_traces, is_middle, 1), (late_traces, is_late, None)),
    )
    return boundary(own, early_held, late_held, from_low, from_high, partial)


def solution(mesh):
    row_split, col_split = P("gx", "gy", None), P(None, "gy", None)
    return jax.shard_map(
        on_device,
        mesh=mesh,
        in_specs=(row_split, P(), col_split) + (P(),) * 8,
        out_specs=row_split,
        check_vma=False,
    )
```

time: 56.9 us -> 37.6 us (0.66)
  the two profiles are of different devices: /device:TPU:15 before, /device:TPU:256 now
where the time goes in v2:
time: 37.6 us; the launch traced here: 37.2 us
  starting transfers between devices  23.1 us (61%)
  Pallas kernels  12.2 us (32%)
  waiting for transfers between devices  1.79 us (5%)
    ppermute x4, starting transfers between devices, move(): return lax.ppermute(x, ('gx', 'gy'), swap(rows, cols, n_y))  21.8 us
    pallas_call x2, Pallas kernels, interior(): pl.pallas_call(kernel, out_shape=outs + [like(x) for x in passed], in_spe...  9.99 us
    ppermute x4, waiting for transfers between devices, move(): return lax.ppermute(x, ('gx', 'gy'), swap(rows, cols, n_y))  1.78 us
    ppermute x2, starting transfers between devices, across(): lax.ppermute(x, ('gx', 'gy'), [(a * n_y + j, b * n_y + j) for a, b in row...  1.32 us
    pallas_call x1, Pallas kernels, boundary(): pl.pallas_call(edge_kernel, out_shape=jax.ShapeDtypeStruct(partial.shape,...  1.13 us
    pallas_call x1, Pallas kernels, packed(): pl.pallas_call(functools.partial(pack_kernel, n_x, n_y), out_shape=[vmem_...  0.99 us
  transfers between devices with their start and end apart: 6, of which 1 were waited for; matrix products, arithmetic and copies ran while one was open for 0% of the time, Pallas kernels for 27%

profile of v2, /device:TPU:256, one launch (start us, length us, event | category | flops | bytes accessed | tf_op | source)
XLA Modules:
  0.0 37.2 jit_solution(2907607940394354283)
XLA Ops:
  0.0 1.0 %own_edges.1 = (f32[4,32,128]{2,1,0:T(8,128)S(1)}, f32[32,128]{1,0:T(8,128)S(1)}, f32[32,128]{1,0:T(8,128)S(1)}, f32[32,128]{1,0:T(8,128)S(1)}, f32[32,128]{1,0:...) custom-call(f32[32,32,128]{2,1,0:T(8,128)} %refs_0_.5, s32[16,4,64]{2,1,0:T(4,128)} %bitcast.4), custom_call_target="tpu_custom_call" | custom-call | tf_op jit(solution)/shard_map/own_edges/pallas_call | solution.py:430
  1.0 0.1 columns_ahead.1
  1.1 0.7 %collective-permute-start.7 = (f32[32,128]{1,0:T(8,128)S(1)}, f32[32,128]{1,0:T(8,128)S(1)}, u32[]{:S(2)}, u32[]{:S(2)}) collective-permute-start(f32[32,128]{1,0:T(8,128)S(1)} %get-tuple-element.77), channel_id=1, source_target_pairs={{448,512},{449,513},{450,514},{451,515},{452,516},{453,517},{454,5... | collective-permute-start | bytes 49160 | tf_op jit(solution)/shard_map/ppermute | solution.py:630
  1.8 23.6 %conditional.2 = ((f32[32,128]{1,0:T(8,128)}, f32[32,128]{1,0:T(8,128)}, f32[32,128]{1,0:T(8,128)}, f32[32,128]{1,0:T(8,128)})) conditional(s32[]{:T(128)} %convert_element_type.6, f32[32,128]{1,0:T(8,128)S(1)} %get-tuple-element.62, (f32[32,128]{1,0:T(8,128)S(1)}, f32[32,128]{1,0:T(8,128)S(1)}, f32[32,128]{1,0:T(8,128)S(1)}, ...), branch_computations={%region_0.1_spmd, %region_1.2_spmd} | conditional | bytes 262344 | solution.py:646
  1.8 1.9 %collective-permute-start = (f32[32,128]{1,0:T(8,128)S(1)}, f32[32,128]{1,0:T(8,128)}, u32[]{:S(2)}, u32[]{:S(2)}) collective-permute-start(f32[32,128]{1,0:T(8,128)S(1)} %get-tuple-element.21), channel_id=1, source_target_pairs={{0,1},{1,0},{2,3},{3,2},{4,5},{5,4},{6,7},{7,6},{8,9},{9,8},{10,11... | collective-permute-start | bytes 49160 | tf_op jit(solution)/shard_map/cond/branch_1_fun/ppermute | solution.py:610
  3.8 8.3 %collective-permute-start.1 = (f32[32,128]{1,0:T(8,128)S(1)}, f32[32,128]{1,0:T(8,128)}, u32[]{:S(2)}, u32[]{:S(2)}) collective-permute-start(f32[32,128]{1,0:T(8,128)S(1)} %get-tuple-element.22), channel_id=1, source_target_pairs={{1,2},{2,1},{3,4},{4,3},{5,6},{6,5},{7,8},{8,7},{9,10},{10,9},{11,... | collective-permute-start | bytes 49160 | tf_op jit(solution)/shard_map/cond/branch_1_fun/ppermute | solution.py:610
  12.0 1.9 %collective-permute-start.2 = (f32[32,128]{1,0:T(8,128)S(1)}, f32[32,128]{1,0:T(8,128)}, u32[]{:S(2)}, u32[]{:S(2)}) collective-permute-start(f32[32,128]{1,0:T(8,128)S(1)} %get-tuple-element.23), channel_id=1, source_target_pairs={{64,128},{128,64},{65,129},{129,65},{66,130},{130,66},{67,131},{13... | collective-permute-start | bytes 49160 | tf_op jit(solution)/shard_map/cond/branch_1_fun/ppermute | solution.py:610
  14.0 9.7 %collective-permute-start.3 = (f32[32,128]{1,0:T(8,128)S(1)}, f32[32,128]{1,0:T(8,128)}, u32[]{:S(2)}, u32[]{:S(2)}) collective-permute-start(f32[32,128]{1,0:T(8,128)S(1)} %get-tuple-element.24), channel_id=1, source_target_pairs={{0,64},{64,0},{1,65},{65,1},{2,66},{66,2},{3,67},{67,3},{4,68},{68... | collective-permute-start | bytes 49160 | tf_op jit(solution)/shard_map/cond/branch_1_fun/ppermute | solution.py:610
  23.6 0.0 collective-permute-done
  23.7 0.0 collective-permute-done.1
  23.7 0.0 collective-permute-done.2
  23.7 1.8 %collective-permute-done.3 = f32[32,128]{1,0:T(8,128)} collective-permute-done((f32[32,128]{1,0:T(8,128)S(1)}, f32[32,128]{1,0:T(8,128)}, u32[]{:S(2)}, u32[]{:S(2)}) %collective-permute-start.3) | collective-permute-done | bytes 16416 | tf_op jit(solution)/shard_map/cond/branch_1_fun/ppermute | solution.py:610
  25.5 0.7 %collective-permute-start.8 = (f32[32,128]{1,0:T(8,128)S(1)}, f32[32,128]{1,0:T(8,128)S(1)}, u32[]{:S(2)}, u32[]{:S(2)}) collective-permute-start(f32[32,128]{1,0:T(8,128)S(1)} %get-tuple-element.78), channel_id=1, source_target_pairs={{512,448},{513,449},{514,450},{515,451},{516,452},{517,453},{518,4... | collective-permute-start | bytes 49160 | tf_op jit(solution)/shard_map/ppermute | solution.py:630
  26.2 9.9 %columns_behind.1 = (f32[32,32,128]{2,1,0:T(8,128)S(1)}, f32[4,32,128]{2,1,0:T(8,128)S(1)}, f32[3,32,128]{2,1,0:T(8,128)S(1)}) custom-call(f32[32,32,128]{2,1,0:T(8,128)} %refs_0_.5, s32[16,1,16]{2,1,0:T(1,128)} %refs_1_.3, bf16[128,1024]{1,0:T(8,128)(2,1)} %refs_2_.3, f32[1,1024]{1,0:T(1,128)} %bitcast.6, ...), custom_call_target="tpu_custom_call", output_to_operand_aliasing={{0}: (10, {}), {1}: (11, {})} | custom-call | flops 1000000000 | bytes 4200000 | tf_op jit(solution)/shard_map/columns_behind/pallas_call | solution.py:498
  36.1 0.0 collective-permute-done.7.from_low
  36.1 0.0 collective-permute-done.8.from_high
  36.1 1.1 %boundary_faces.1 = f32[32,32,128]{2,1,0:T(8,128)} custom-call(f32[4,32,128]{2,1,0:T(8,128)S(1)} %get-tuple-element.54.edges, f32[4,32,128]{2,1,0:T(8,128)S(1)} %get-tuple-element.75.early, f32[3,32,128]{2,1,0:T(8,128)S(1)} %get-tuple-element.76.late, f32[32,128]{1,0:T(8,128)S(1)} %collective-permute-done.7.from_low, ...), custom_call_target="tpu_custom_call" | custom-call | flops 2000000 | bytes 600000 | tf_op jit(solution)/shard_map/boundary_faces/pallas_call | solution.py:547
  (3 shorter events, 0.1 us)
Async XLA Ops:
  1.1 34.9 %collective-permute-start.7 = (f32[32,128]{1,0:T(8,128)S(1)}, f32[32,128]{1,0:T(8,128)S(1)}, u32[]{:S(2)}, u32[]{:S(2)}) collective-permute-start(f32[32,128]{1,0:T(8,128)S(1)} %get-tuple-element.77), channel_id=1, source_target_pairs={{448,512},{449,513},{450,514},{451,515},{452,516},{453,517},{454,5... | collective-permute-start | bytes 49160 | tf_op jit(solution)/shard_map/ppermute | solution.py:630
  1.8 21.8 %collective-permute-start = (f32[32,128]{1,0:T(8,128)S(1)}, f32[32,128]{1,0:T(8,128)}, u32[]{:S(2)}, u32[]{:S(2)}) collective-permute-start(f32[32,128]{1,0:T(8,128)S(1)} %get-tuple-element.21), channel_id=1, source_target_pairs={{0,1},{1,0},{2,3},{3,2},{4,5},{5,4},{6,7},{7,6},{8,9},{9,8},{10,11... | collective-permute-start | bytes 49160 | tf_op jit(solution)/shard_map/cond/branch_1_fun/ppermute | solution.py:610
  3.8 19.9 %collective-permute-start.1 = (f32[32,128]{1,0:T(8,128)S(1)}, f32[32,128]{1,0:T(8,128)}, u32[]{:S(2)}, u32[]{:S(2)}) collective-permute-start(f32[32,128]{1,0:T(8,128)S(1)} %get-tuple-element.22), channel_id=1, source_target_pairs={{1,2},{2,1},{3,4},{4,3},{5,6},{6,5},{7,8},{8,7},{9,10},{10,9},{11,... | collective-permute-start | bytes 49160 | tf_op jit(solution)/shard_map/cond/branch_1_fun/ppermute | solution.py:610
  12.0 11.6 %collective-permute-start.2 = (f32[32,128]{1,0:T(8,128)S(1)}, f32[32,128]{1,0:T(8,128)}, u32[]{:S(2)}, u32[]{:S(2)}) collective-permute-start(f32[32,128]{1,0:T(8,128)S(1)} %get-tuple-element.23), channel_id=1, source_target_pairs={{64,128},{128,64},{65,129},{129,65},{66,130},{130,66},{67,131},{13... | collective-permute-start | bytes 49160 | tf_op jit(solution)/shard_map/cond/branch_1_fun/ppermute | solution.py:610
  14.0 11.5 %collective-permute-start.3 = (f32[32,128]{1,0:T(8,128)S(1)}, f32[32,128]{1,0:T(8,128)}, u32[]{:S(2)}, u32[]{:S(2)}) collective-permute-start(f32[32,128]{1,0:T(8,128)S(1)} %get-tuple-element.24), channel_id=1, source_target_pairs={{0,64},{64,0},{1,65},{65,1},{2,66},{66,2},{3,67},{67,3},{4,68},{68... | collective-permute-start | bytes 49160 | tf_op jit(solution)/shard_map/cond/branch_1_fun/ppermute | solution.py:610
  25.5 10.6 %collective-permute-start.8 = (f32[32,128]{1,0:T(8,128)S(1)}, f32[32,128]{1,0:T(8,128)S(1)}, u32[]{:S(2)}, u32[]{:S(2)}) collective-permute-start(f32[32,128]{1,0:T(8,128)S(1)} %get-tuple-element.78), channel_id=1, source_target_pairs={{512,448},{513,449},{514,450},{515,451},{516,452},{517,453},{518,4... | collective-permute-start | bytes 49160 | tf_op jit(solution)/shard_map/ppermute | solution.py:630

commit v3 on v2

--- a/solution.py
+++ b/solution.py
@@ -113,7 +113,7 @@
 
 
 def ahead(row, col):
-    return (row % WRAP == 0) & ((row > 0) | (col > 0))
+    return ((row % WRAP == 0) & ((row > 0) | (col > 0))) | ((row == 1) & (col == 0))
 
 
 def turned(edge):
@@ -129,7 +129,7 @@
     return jnp.concatenate(pieces, axis=0)
 
 
-def pack_kernel(n_x, n_y, air, edge_map, own, wrap, row_even, row_odd, col_even, col_odd, back, maps, sems):
+def pack_kernel(n_x, n_y, air, edge_map, own, late_even, wrap, row_even, row_odd, col_even, col_odd, back, maps, sems):
     rows, cols, _ = air.shape
     row, col = lax.axis_index("gx"), lax.axis_index("gy")
     west, east = (row + n_x - 1) % n_x, (row + 1) % n_x
@@ -159,6 +159,7 @@
     even = row % 2 == 0
     row_even[...] = jnp.where(even, to_east, to_west)
     odd = jnp.where(even, to_west, to_east)
+    late_even[...] = row_even[...]
     row_odd[...] = odd
     wrap[...] = odd
     back[...] = odd
@@ -168,7 +169,7 @@
 
 
 def main_kernel(early, inputs, moved, result, scratch):
-    held, sems, move_sems, normed, base, listed, fields, total = scratch
+    held, sems, move_sems, normed, base, listed, fields = scratch
     row = lax.axis_index("gx")
     col = lax.axis_index("gy")
     moves = start_moves(moved, move_sems, row)
@@ -187,10 +188,7 @@
             for k in numbers:
                 copies[k].wait()
 
-        columns_and_interior(held, ready, normed, base, listed, fields, total)
-        end = pltpu.make_async_copy(total, result, sems.at[0])
-        end.start()
-        end.wait()
+        columns_and_interior(held, ready, normed, base, listed, fields, result)
 
     end_moves(moves, row)
 
@@ -263,17 +261,27 @@
     def _():
         ready(4, 5, 7, 8, 9)
 
-    def land_group(g, carry):
-        numbers = [listed[g * GROUP + k] for k in range(GROUP)]
-        starts = [pl.multiple_of(t * TILE, TILE) for t in numbers]
+    def land_group(first, count):
+        starts = [pl.multiple_of(listed[first + k] * TILE, TILE) for k in range(count)]
         normed = jnp.concatenate([normed_ref[pl.ds(s, TILE), :] for s in starts], axis=0)
         land = silu(dot(normed, land_in[...]) + land_b[...])
         term = two_layers(land, mid_w, mid_b, land_out)
         for k, s in enumerate(starts):
             base[pl.ds(s, TILE), :] = base[pl.ds(s, TILE), :] + term[k * TILE : (k + 1) * TILE]
+
+    def whole_group(g, carry):
+        land_group(g * GROUP, GROUP)
         return carry
 
-    lax.fori_loop(0, (lands + GROUP - 1) // GROUP, land_group, 0)
+    half = GROUP // 2
+    over = lands % GROUP
+    whole = lands // GROUP + jnp.where(over > half, 1, 0)
+    lax.fori_loop(0, whole, whole_group, 0)
+
+    @pl.when((over > 0) & (over <= half))
+    def _():
+        land_group(whole * GROUP, half)
+
     interior_and_sum(air, fields, base, out)
 
     @pl.when(lands == 0)
@@ -430,9 +438,9 @@
     return pl.pallas_call(
         functools.partial(pack_kernel, n_x, n_y),
         out_shape=[vmem_array((4, cols, feat), jnp.float32)]
-        + [vmem_array((cols, feat), jnp.float32)] * 6,
+        + [vmem_array((cols, feat), jnp.float32)] * 7,
         in_specs=[in_hbm()] * 2,
-        out_specs=[in_vmem()] * 7,
+        out_specs=[in_vmem()] * 8,
         scratch_shapes=[
             pltpu.SMEM((3,) + edge_map.shape[1:], jnp.int32),
             pltpu.SemaphoreType.DMA((7,)),
@@ -510,7 +518,6 @@
             pltpu.VMEM((rows * cols + TILE, feat), jnp.float32),
             pltpu.SMEM((tiles + GROUP,), jnp.int32),
             pltpu.VMEM((6, rows, 4, cols // 4, feat), jnp.float32),
-            pltpu.VMEM(air_state.shape, jnp.float32),
         ],
         input_output_aliases=aliases,
         compiler_params=pltpu.CompilerParams(vmem_limit_bytes=32 * 1024 * 1024),
@@ -618,13 +625,12 @@
             move(row_even, [p for p in evens if p[1] not in late], col_same),
         )
 
-    def exchange_late(row_even, col_odd, col_even):
+    def exchange_late_cols(col_odd, col_even):
         same = [(i, i) for i in late]
-        return (
-            move(col_even, same, col_evens),
-            move(col_odd, same, col_odds),
-            move(row_even, [p for p in evens if p[1] in late], col_same),
-        )
+        return move(col_even, same, col_evens), move(col_odd, same, col_odds)
+
+    def exchange_late_rows(row_even):
+        return (move(row_even, [p for p in evens if p[1] in late], col_same),)
 
     def across(x, rows):
         return lax.ppermute(
@@ -636,7 +642,7 @@
     is_first = lambda r: r % WRAP == 0
     is_middle = lambda r: (r % WRAP > 0) & (r % WRAP < WRAP - 1)
     is_late = lambda r: r % WRAP >= WRAP - 2
-    own, wrap, row_even, row_odd, col_even, col_odd, back = packed(
+    own, late_even, wrap, row_even, row_odd, col_even, col_odd, back = packed(
         air_state, edge_map.transpose(0, 2, 1), n_x, n_y
     )
     partial, wrap, row_even, row_odd, col_even, col_odd, back = interior(
@@ -646,17 +652,18 @@
     early_traces = lax.cond(
         place < WRAP - 1, exchange_early, nothing(4), row_even, row_odd, col_odd, col_even
     )
-    early_held, back = collected(early_traces, is_first, (back,))
+    early_held, back, late_even = collected(early_traces, is_first, (back, late_even))
     from_high = across(back, [(b, a) for a, b in wraps])
-    late_traces = lax.cond(
-        place >= WRAP - 2, exchange_late, nothing(3), row_even, col_odd, col_even
-    )
+    late_cols = lax.cond(
+        place == WRAP - 1, exchange_late_cols, nothing(2), col_odd, col_even
+    )
+    late_rows = lax.cond(place >= WRAP - 2, exchange_late_rows, nothing(1), late_even)
     partial, early_held, late_held = interior(
         False,
         inputs,
         (),
         (partial, early_held),
-        ((early_traces, is_middle, 1), (late_traces, is_late, None)),
+        ((early_traces, is_middle, 1), ((*late_cols, *late_rows), is_late, None)),
     )
     return boundary(own, early_held, late_held, from_low, from_high, partial)
 

time: 37.6 us -> 36.4 us (0.968)
  the two profiles are of different devices: /device:TPU:256 before, /device:TPU:384 now
where the time goes in v3:
time: 36.4 us; the launch traced here: 36 us
  starting transfers between devices  19.8 us (54%)
  Pallas kernels  12.1 us (33%)
  waiting for transfers between devices  3.79 us (10%)
    ppermute x4, starting transfers between devices, move(): return lax.ppermute(x, ('gx', 'gy'), swap(rows, cols, n_y))  18.5 us
    pallas_call x2, Pallas kernels, interior(): pl.pallas_call(kernel, out_shape=outs + [like(x) for x in passed], in_spe...  9.96 us
    ppermute x4, waiting for transfers between devices, move(): return lax.ppermute(x, ('gx', 'gy'), swap(rows, cols, n_y))  3.79 us
    ppermute x2, starting transfers between devices, across(): lax.ppermute(x, ('gx', 'gy'), [(a * n_y + j, b * n_y + j) for a, b in row...  1.32 us
    pallas_call x1, Pallas kernels, boundary(): pl.pallas_call(edge_kernel, out_shape=jax.ShapeDtypeStruct(partial.shape,...  1.13 us
    pallas_call x1, Pallas kernels, packed(): pl.pallas_call(functools.partial(pack_kernel, n_x, n_y), out_shape=[vmem_...  0.99 us
  transfers between devices with their start and end apart: 6, of which 1 were waited for; matrix products, arithmetic and copies ran while one was open for 0% of the time, Pallas kernels for 27%

profile of v3, /device:TPU:384, one launch (start us, length us, event | category | flops | bytes accessed | tf_op | source)
XLA Modules:
  0.0 36.0 jit_solution(10225871218601618435)
XLA Ops:
  0.0 1.0 %own_edges.1 = (f32[4,32,128]{2,1,0:T(8,128)S(1)}, f32[32,128]{1,0:T(8,128)S(1)}, f32[32,128]{1,0:T(8,128)S(1)}, f32[32,128]{1,0:T(8,128)S(1)}, f32[32,128]{1,0:...) custom-call(f32[32,32,128]{2,1,0:T(8,128)} %refs_0_.6, s32[16,4,64]{2,1,0:T(4,128)} %bitcast.4), custom_call_target="tpu_custom_call" | custom-call | tf_op jit(solution)/shard_map/own_edges/pallas_call | solution.py:438
  1.0 0.1 columns_ahead.1
  1.1 0.7 %collective-permute-start.7 = (f32[32,128]{1,0:T(8,128)S(1)}, f32[32,128]{1,0:T(8,128)S(1)}, u32[]{:S(2)}, u32[]{:S(2)}) collective-permute-start(f32[32,128]{1,0:T(8,128)S(1)} %get-tuple-element.81), channel_id=1, source_target_pairs={{448,512},{449,513},{450,514},{451,515},{452,516},{453,517},{454,5... | collective-permute-start | bytes 49160 | tf_op jit(solution)/shard_map/ppermute | solution.py:636
  1.8 22.4 %conditional.3 = ((f32[32,128]{1,0:T(8,128)}, f32[32,128]{1,0:T(8,128)}, f32[32,128]{1,0:T(8,128)}, f32[32,128]{1,0:T(8,128)})) conditional(s32[]{:T(128)} %convert_element_type.9, f32[32,128]{1,0:T(8,128)S(1)} %get-tuple-element.65, (f32[32,128]{1,0:T(8,128)S(1)}, f32[32,128]{1,0:T(8,128)S(1)}, f32[32,128]{1,0:T(8,128)S(1)}, ...), branch_computations={%region_0.1_spmd, %region_1.2_spmd} | conditional | bytes 262344 | solution.py:652
  1.8 1.9 %collective-permute-start = (f32[32,128]{1,0:T(8,128)S(1)}, f32[32,128]{1,0:T(8,128)}, u32[]{:S(2)}, u32[]{:S(2)}) collective-permute-start(f32[32,128]{1,0:T(8,128)S(1)} %get-tuple-element.24), channel_id=1, source_target_pairs={{0,1},{1,0},{2,3},{3,2},{4,5},{5,4},{6,7},{7,6},{8,9},{9,8},{10,11... | collective-permute-start | bytes 49160 | tf_op jit(solution)/shard_map/cond/branch_1_fun/ppermute | solution.py:617
  3.8 8.3 %collective-permute-start.1 = (f32[32,128]{1,0:T(8,128)S(1)}, f32[32,128]{1,0:T(8,128)}, u32[]{:S(2)}, u32[]{:S(2)}) collective-permute-start(f32[32,128]{1,0:T(8,128)S(1)} %get-tuple-element.25), channel_id=1, source_target_pairs={{1,2},{2,1},{3,4},{4,3},{5,6},{6,5},{7,8},{8,7},{9,10},{10,9},{11,... | collective-permute-start | bytes 49160 | tf_op jit(solution)/shard_map/cond/branch_1_fun/ppermute | solution.py:617
  12.0 6.4 %collective-permute-start.2 = (f32[32,128]{1,0:T(8,128)S(1)}, f32[32,128]{1,0:T(8,128)}, u32[]{:S(2)}, u32[]{:S(2)}) collective-permute-start(f32[32,128]{1,0:T(8,128)S(1)} %get-tuple-element.26), channel_id=1, source_target_pairs={{64,128},{128,64},{65,129},{129,65},{66,130},{130,66},{67,131},{13... | collective-permute-start | bytes 49160 | tf_op jit(solution)/shard_map/cond/branch_1_fun/ppermute | solution.py:617
  18.4 1.9 %collective-permute-start.3 = (f32[32,128]{1,0:T(8,128)S(1)}, f32[32,128]{1,0:T(8,128)}, u32[]{:S(2)}, u32[]{:S(2)}) collective-permute-start(f32[32,128]{1,0:T(8,128)S(1)} %get-tuple-element.27), channel_id=1, source_target_pairs={{0,64},{64,0},{1,65},{65,1},{2,66},{66,2},{3,67},{67,3},{4,68},{68... | collective-permute-start | bytes 49160 | tf_op jit(solution)/shard_map/cond/branch_1_fun/ppermute | solution.py:617
  20.4 0.0 collective-permute-done
  20.4 0.0 collective-permute-done.1
  20.4 0.0 collective-permute-done.2
  20.4 3.8 %collective-permute-done.3 = f32[32,128]{1,0:T(8,128)} collective-permute-done((f32[32,128]{1,0:T(8,128)S(1)}, f32[32,128]{1,0:T(8,128)}, u32[]{:S(2)}, u32[]{:S(2)}) %collective-permute-start.3) | collective-permute-done | bytes 16416 | tf_op jit(solution)/shard_map/cond/branch_1_fun/ppermute | solution.py:617
  24.2 0.7 %collective-permute-start.8 = (f32[32,128]{1,0:T(8,128)S(1)}, f32[32,128]{1,0:T(8,128)S(1)}, u32[]{:S(2)}, u32[]{:S(2)}) collective-permute-start(f32[32,128]{1,0:T(8,128)S(1)} %get-tuple-element.82), channel_id=1, source_target_pairs={{512,448},{513,449},{514,450},{515,451},{516,452},{517,453},{518,4... | collective-permute-start | bytes 49160 | tf_op jit(solution)/shard_map/ppermute | solution.py:636
  25.0 9.8 %columns_behind.1 = (f32[32,32,128]{2,1,0:T(8,128)S(1)}, f32[4,32,128]{2,1,0:T(8,128)S(1)}, f32[3,32,128]{2,1,0:T(8,128)S(1)}) custom-call(f32[32,32,128]{2,1,0:T(8,128)} %refs_0_.6, s32[16,1,16]{2,1,0:T(1,128)} %refs_1_.3, bf16[128,1024]{1,0:T(8,128)(2,1)} %refs_2_.3, f32[1,1024]{1,0:T(1,128)} %bitcast.6, ...), custom_call_target="tpu_custom_call", output_to_operand_aliasing={{0}: (10, {}), {1}: (11, {})} | custom-call | flops 1000000000 | bytes 4200000 | tf_op jit(solution)/shard_map/columns_behind/pallas_call | solution.py:506
  34.8 0.0 collective-permute-done.7.from_low
  34.8 0.0 collective-permute-done.8.from_high
  34.8 1.1 %boundary_faces.1 = f32[32,32,128]{2,1,0:T(8,128)} custom-call(f32[4,32,128]{2,1,0:T(8,128)S(1)} %get-tuple-element.57.edges, f32[4,32,128]{2,1,0:T(8,128)S(1)} %get-tuple-element.79.early, f32[3,32,128]{2,1,0:T(8,128)S(1)} %get-tuple-element.80.late, f32[32,128]{1,0:T(8,128)S(1)} %collective-permute-done.7.from_low, ...), custom_call_target="tpu_custom_call" | custom-call | flops 2000000 | bytes 600000 | tf_op jit(solution)/shard_map/boundary_faces/pallas_call | solution.py:554
  (5 shorter events, 0.1 us)
Async XLA Ops:
  1.1 33.7 %collective-permute-start.7 = (f32[32,128]{1,0:T(8,128)S(1)}, f32[32,128]{1,0:T(8,128)S(1)}, u32[]{:S(2)}, u32[]{:S(2)}) collective-permute-start(f32[32,128]{1,0:T(8,128)S(1)} %get-tuple-element.81), channel_id=1, source_target_pairs={{448,512},{449,513},{450,514},{451,515},{452,516},{453,517},{454,5... | collective-permute-start | bytes 49160 | tf_op jit(solution)/shard_map/ppermute | solution.py:636
  1.8 18.5 %collective-permute-start = (f32[32,128]{1,0:T(8,128)S(1)}, f32[32,128]{1,0:T(8,128)}, u32[]{:S(2)}, u32[]{:S(2)}) collective-permute-start(f32[32,128]{1,0:T(8,128)S(1)} %get-tuple-element.24), channel_id=1, source_target_pairs={{0,1},{1,0},{2,3},{3,2},{4,5},{5,4},{6,7},{7,6},{8,9},{9,8},{10,11... | collective-permute-start | bytes 49160 | tf_op jit(solution)/shard_map/cond/branch_1_fun/ppermute | solution.py:617
  3.8 16.6 %collective-permute-start.1 = (f32[32,128]{1,0:T(8,128)S(1)}, f32[32,128]{1,0:T(8,128)}, u32[]{:S(2)}, u32[]{:S(2)}) collective-permute-start(f32[32,128]{1,0:T(8,128)S(1)} %get-tuple-element.25), channel_id=1, source_target_pairs={{1,2},{2,1},{3,4},{4,3},{5,6},{6,5},{7,8},{8,7},{9,10},{10,9},{11,... | collective-permute-start | bytes 49160 | tf_op jit(solution)/shard_map/cond/branch_1_fun/ppermute | solution.py:617
  12.0 8.4 %collective-permute-start.2 = (f32[32,128]{1,0:T(8,128)S(1)}, f32[32,128]{1,0:T(8,128)}, u32[]{:S(2)}, u32[]{:S(2)}) collective-permute-start(f32[32,128]{1,0:T(8,128)S(1)} %get-tuple-element.26), channel_id=1, source_target_pairs={{64,128},{128,64},{65,129},{129,65},{66,130},{130,66},{67,131},{13... | collective-permute-start | bytes 49160 | tf_op jit(solution)/shard_map/cond/branch_1_fun/ppermute | solution.py:617
  18.4 5.7 %collective-permute-start.3 = (f32[32,128]{1,0:T(8,128)S(1)}, f32[32,128]{1,0:T(8,128)}, u32[]{:S(2)}, u32[]{:S(2)}) collective-permute-start(f32[32,128]{1,0:T(8,128)S(1)} %get-tuple-element.27), channel_id=1, source_target_pairs={{0,64},{64,0},{1,65},{65,1},{2,66},{66,2},{3,67},{67,3},{4,68},{68... | collective-permute-start | bytes 49160 | tf_op jit(solution)/shard_map/cond/branch_1_fun/ppermute | solution.py:617
  24.2 10.6 %collective-permute-start.8 = (f32[32,128]{1,0:T(8,128)S(1)}, f32[32,128]{1,0:T(8,128)S(1)}, u32[]{:S(2)}, u32[]{:S(2)}) collective-permute-start(f32[32,128]{1,0:T(8,128)S(1)} %get-tuple-element.82), channel_id=1, source_target_pairs={{512,448},{513,449},{514,450},{515,451},{516,452},{517,453},{518,4... | collective-permute-start | bytes 49160 | tf_op jit(solution)/shard_map/ppermute | solution.py:636

commit v4 on v3

--- a/solution.py
+++ b/solution.py
@@ -129,7 +129,7 @@
     return jnp.concatenate(pieces, axis=0)
 
 
-def pack_kernel(n_x, n_y, air, edge_map, own, late_even, wrap, row_even, row_odd, col_even, col_odd, back, maps, sems):
+def pack_kernel(n_x, n_y, air, edge_map, own, late_even, wrap, row_even, col_even, col_odd, back, maps, sems):
     rows, cols, _ = air.shape
     row, col = lax.axis_index("gx"), lax.axis_index("gy")
     west, east = (row + n_x - 1) % n_x, (row + 1) % n_x
@@ -160,11 +160,12 @@
     row_even[...] = jnp.where(even, to_east, to_west)
     odd = jnp.where(even, to_west, to_east)
     late_even[...] = row_even[...]
-    row_odd[...] = odd
-    wrap[...] = odd
     back[...] = odd
     even = col % 2 == 0
-    col_even[...] = jnp.where(even, to_north, to_south)
+    paired = jnp.where(even, to_north, to_south)
+    col_even[...] = paired
+    beside = (row % WRAP == 0) | (row % WRAP == WRAP - 1)
+    wrap[...] = jnp.where(beside, odd, paired)
     col_odd[...] = jnp.where(even, to_south, to_north)
 
 
@@ -358,7 +359,7 @@
 
 
 def edge_kernel(edges, early, late, from_low, from_high, partial, out, low, high, top, bottom, sems):
-    col_even_a, col_odd_a, row_odd_a, row_even_a = (early[k] for k in range(4))
+    col_odd_a, row_even_a, col_even_first = (early[k] for k in range(3))
     col_even_b, col_odd_b, row_even_b = (late[k] for k in range(3))
     rows, cols, feat = out.shape
     first, middle, final = pl.ds(0, 8), pl.ds(8, cols - 16), pl.ds(cols - 8, 8)
@@ -369,12 +370,12 @@
     place = row % WRAP
     last_row = place == WRAP - 1
     first_x = jnp.where(place < WRAP - 2, row_even_a, row_even_b)
-    wrapped = jnp.where(place == 0, from_low[...], from_high[...])
-    second_x = jnp.where((place == 0) | last_row, wrapped, row_odd_a)
+    second_x = jnp.where(place == 0, from_low[...], from_high[...])
     even = row % 2 == 0
     west = jnp.where(even, second_x, first_x)
     east = jnp.where(even, first_x, second_x)
-    first_y = jnp.where(last_row, col_even_b, col_even_a)
+    first_y = jnp.where(place == 0, col_even_first, from_low[...])
+    first_y = jnp.where(last_row, col_even_b, first_y)
     second_y = jnp.where(last_row, col_odd_b, col_odd_a)
     even = col % 2 == 0
     south = jnp.where(even, second_y, first_y)
@@ -438,9 +439,9 @@
     return pl.pallas_call(
         functools.partial(pack_kernel, n_x, n_y),
         out_shape=[vmem_array((4, cols, feat), jnp.float32)]
-        + [vmem_array((cols, feat), jnp.float32)] * 7,
+        + [vmem_array((cols, feat), jnp.float32)] * 6,
         in_specs=[in_hbm()] * 2,
-        out_specs=[in_vmem()] * 8,
+        out_specs=[in_vmem()] * 7,
         scratch_shapes=[
             pltpu.SMEM((3,) + edge_map.shape[1:], jnp.int32),
             pltpu.SemaphoreType.DMA((7,)),
@@ -607,6 +608,8 @@
     row = lax.axis_index("gx")
     late = [i for i in range(n_x) if i % WRAP == WRAP - 1]
     early = [i for i in range(n_x) if i not in late]
+    first = [i for i in early if i % WRAP == 0]
+    inner = [i for i in early if i not in first]
     evens = [(i, i + 1) for i in range(0, n_x, 2)]
     odds = [(i, (i + 1) % n_x) for i in range(1, n_x, 2)]
     col_evens = [(j, j + 1) for j in range(0, n_y, 2)]
@@ -616,14 +619,15 @@
     def move(x, rows, cols):
         return lax.ppermute(x, ("gx", "gy"), swap(rows, cols, n_y))
 
-    def exchange_early(row_even, row_odd, col_odd, col_even):
+    def exchange_early(col_odd, row_even):
         same = [(i, i) for i in early]
         return (
-            move(col_even, same, col_evens),
             move(col_odd, same, col_odds),
-            move(row_odd, [p for p in odds if p[0] not in late], col_same),
             move(row_even, [p for p in evens if p[1] not in late], col_same),
         )
+
+    def exchange_first(col_even):
+        return (move(col_even, [(i, i) for i in first], col_evens),)
 
     def exchange_late_cols(col_odd, col_even):
         same = [(i, i) for i in late]
@@ -632,28 +636,29 @@
     def exchange_late_rows(row_even):
         return (move(row_even, [p for p in evens if p[1] in late], col_same),)
 
-    def across(x, rows):
-        return lax.ppermute(
-            x, ("gx", "gy"), [(a * n_y + j, b * n_y + j) for a, b in rows for j in range(n_y)]
-        )
+    def across(x, rows, others, cols):
+        pairs = [(a * n_y + j, b * n_y + j) for a, b in rows for j in range(n_y)]
+        return lax.ppermute(x, ("gx", "gy"), pairs + swap(others, cols, n_y))
 
     place = row % WRAP
     wraps = [p for p in odds if p[0] in late]
     is_first = lambda r: r % WRAP == 0
     is_middle = lambda r: (r % WRAP > 0) & (r % WRAP < WRAP - 1)
     is_late = lambda r: r % WRAP >= WRAP - 2
-    own, late_even, wrap, row_even, row_odd, col_even, col_odd, back = packed(
+    own, late_even, wrap, row_even, col_even, col_odd, back = packed(
         air_state, edge_map.transpose(0, 2, 1), n_x, n_y
     )
-    partial, wrap, row_even, row_odd, col_even, col_odd, back = interior(
-        True, inputs, (wrap, row_even, row_odd, col_even, col_odd, back)
-    )
-    from_low = across(wrap, wraps)
-    early_traces = lax.cond(
-        place < WRAP - 1, exchange_early, nothing(4), row_even, row_odd, col_odd, col_even
-    )
+    partial, wrap, row_even, col_even, col_odd, back = interior(
+        True, inputs, (wrap, row_even, col_even, col_odd, back)
+    )
+    from_low = across(wrap, wraps, [(i, i) for i in inner], col_evens)
+    first_traces = lax.cond(place == 0, exchange_first, nothing(1), col_even)
+    early_traces = lax.cond(place < WRAP - 1, exchange_early, nothing(2), col_odd, row_even)
+    early_traces = (*early_traces, *first_traces)
     early_held, back, late_even = collected(early_traces, is_first, (back, late_even))
-    from_high = across(back, [(b, a) for a, b in wraps])
+    from_high = across(
+        back, [(b, a) for a, b in wraps], [p for p in odds if p[0] not in late], col_same
+    )
     late_cols = lax.cond(
         place == WRAP - 1, exchange_late_cols, nothing(2), col_odd, col_even
     )

time: 36.4 us -> 35.4 us (0.973)
  starting transfers between devices: 19.8 us -> 18.9 us
    ppermute x4 -> x2, starting transfers between devices: 18.5 us -> 10.2 us  [move(): return lax.ppermute(x, ('gx', 'gy'), swap(rows, cols, n_y))]
    ppermute x2, starting transfers between devices: 1.32 us -> 8.69 us  [across(): return lax.ppermute(x, ('gx', 'gy'), pairs + swap(others, cols, n_y))]
    ppermute x4 -> x2, waiting for transfers between devices: 3.79 us -> 3.8 us  [move(): return lax.ppermute(x, ('gx', 'gy'), swap(rows, cols, n_y))]
  transfers between devices with their start and end apart: 6 -> 4, of which waited for: 1 -> 1; matrix products, arithmetic and copies ran while one was open for 0% -> 0% of each run, Pallas kernels for 27% -> 28%
where the time goes in v4:
time: 35.4 us; the launch traced here: 34.9 us
  starting transfers between devices  18.9 us (53%)
  Pallas kernels  12.1 us (34%)
  waiting for transfers between devices  3.81 us (11%)
    ppermute x2, starting transfers between devices, move(): return lax.ppermute(x, ('gx', 'gy'), swap(rows, cols, n_y))  10.2 us
    pallas_call x2, Pallas kernels, interior(): pl.pallas_call(kernel, out_shape=outs + [like(x) for x in passed], in_spe...  9.93 us
    ppermute x2, starting transfers between devices, across(): return lax.ppermute(x, ('gx', 'gy'), pairs + swap(others, cols, n_y))  8.69 us
    ppermute x2, waiting for transfers between devices, move(): return lax.ppermute(x, ('gx', 'gy'), swap(rows, cols, n_y))  3.8 us
    pallas_call x1, Pallas kernels, boundary(): pl.pallas_call(edge_kernel, out_shape=jax.ShapeDtypeStruct(partial.shape,...  1.13 us
    pallas_call x1, Pallas kernels, packed(): pl.pallas_call(functools.partial(pack_kernel, n_x, n_y), out_shape=[vmem_...  0.99 us
  transfers between devices with their start and end apart: 4, of which 1 were waited for; matrix products, arithmetic and copies ran while one was open for 0% of the time, Pallas kernels for 28%

profile of v4, /device:TPU:384, one launch (start us, length us, event | category | flops | bytes accessed | tf_op | source)
XLA Modules:
  0.0 34.9 jit_solution(10896736141815643705)
XLA Ops:
  0.0 1.0 %own_edges.1 = (f32[4,32,128]{2,1,0:T(8,128)S(1)}, f32[32,128]{1,0:T(8,128)S(1)}, f32[32,128]{1,0:T(8,128)S(1)}, f32[32,128]{1,0:T(8,128)S(1)}, f32[32,128]{1,0:...) custom-call(f32[32,32,128]{2,1,0:T(8,128)} %refs_0_.7, s32[16,4,64]{2,1,0:T(4,128)} %bitcast.4), custom_call_target="tpu_custom_call" | custom-call | tf_op jit(solution)/shard_map/own_edges/pallas_call | solution.py:439
  1.0 0.1 columns_ahead.1
  1.1 1.9 %collective-permute-start.6 = (f32[32,128]{1,0:T(8,128)S(1)}, f32[32,128]{1,0:T(8,128)S(1)}, u32[]{:S(2)}, u32[]{:S(2)}) collective-permute-start(f32[32,128]{1,0:T(8,128)S(1)} %get-tuple-element.72), channel_id=1, source_target_pairs={{448,512},{449,513},{450,514},{451,515},{452,516},{453,517},{454,5... | collective-permute-start | bytes 49160 | tf_op jit(solution)/shard_map/ppermute | solution.py:641
  3.1 14.0 %conditional.4 = ((f32[32,128]{1,0:T(8,128)}, f32[32,128]{1,0:T(8,128)})) conditional(s32[]{:T(128)} %convert_element_type.12, f32[32,128]{1,0:T(8,128)S(1)} %get-tuple-element.59, (f32[32,128]{1,0:T(8,128)S(1)}, f32[32,128]{1,0:T(8,128)S(1)}) %tuple.31), branch_computations={%region_0.1_spmd, %region_1.2_spmd} | conditional | bytes 131176 | solution.py:656
  3.1 8.3 %collective-permute-start = (f32[32,128]{1,0:T(8,128)S(1)}, f32[32,128]{1,0:T(8,128)}, u32[]{:S(2)}, u32[]{:S(2)}) collective-permute-start(f32[32,128]{1,0:T(8,128)S(1)} %get-tuple-element.25), channel_id=1, source_target_pairs={{1,2},{2,1},{3,4},{4,3},{5,6},{6,5},{7,8},{8,7},{9,10},{10,9},{11,... | collective-permute-start | bytes 49160 | tf_op jit(solution)/shard_map/cond/branch_1_fun/ppermute | solution.py:620
  11.4 1.9 %collective-permute-start.1 = (f32[32,128]{1,0:T(8,128)S(1)}, f32[32,128]{1,0:T(8,128)}, u32[]{:S(2)}, u32[]{:S(2)}) collective-permute-start(f32[32,128]{1,0:T(8,128)S(1)} %get-tuple-element.26), channel_id=1, source_target_pairs={{0,64},{64,0},{1,65},{65,1},{2,66},{66,2},{3,67},{67,3},{4,68},{68... | collective-permute-start | bytes 49160 | tf_op jit(solution)/shard_map/cond/branch_1_fun/ppermute | solution.py:620
  13.3 0.0 collective-permute-done
  13.3 3.8 %collective-permute-done.1 = f32[32,128]{1,0:T(8,128)} collective-permute-done((f32[32,128]{1,0:T(8,128)S(1)}, f32[32,128]{1,0:T(8,128)}, u32[]{:S(2)}, u32[]{:S(2)}) %collective-permute-start.1) | collective-permute-done | bytes 16416 | tf_op jit(solution)/shard_map/cond/branch_1_fun/ppermute | solution.py:620
  17.1 6.8 %collective-permute-start.7 = (f32[32,128]{1,0:T(8,128)S(1)}, f32[32,128]{1,0:T(8,128)S(1)}, u32[]{:S(2)}, u32[]{:S(2)}) collective-permute-start(f32[32,128]{1,0:T(8,128)S(1)} %get-tuple-element.73), channel_id=1, source_target_pairs={{512,448},{513,449},{514,450},{515,451},{516,452},{517,453},{518,4... | collective-permute-start | bytes 49160 | tf_op jit(solution)/shard_map/ppermute | solution.py:641
  24.0 9.8 %columns_behind.1 = (f32[32,32,128]{2,1,0:T(8,128)S(1)}, f32[3,32,128]{2,1,0:T(8,128)S(1)}, f32[3,32,128]{2,1,0:T(8,128)S(1)}) custom-call(f32[32,32,128]{2,1,0:T(8,128)} %refs_0_.7, s32[16,1,16]{2,1,0:T(1,128)} %refs_1_.3, bf16[128,1024]{1,0:T(8,128)(2,1)} %refs_2_.3, f32[1,1024]{1,0:T(1,128)} %bitcast.6, ...), custom_call_target="tpu_custom_call", output_to_operand_aliasing={{0}: (10, {}), {1}: (11, {})} | custom-call | flops 1000000000 | bytes 4200000 | tf_op jit(solution)/shard_map/columns_behind/pallas_call | solution.py:507
  33.8 0.0 collective-permute-done.6.from_low
  33.8 0.0 collective-permute-done.7.from_high
  33.8 1.1 %boundary_faces.1 = f32[32,32,128]{2,1,0:T(8,128)} custom-call(f32[4,32,128]{2,1,0:T(8,128)S(1)} %get-tuple-element.52.edges, f32[3,32,128]{2,1,0:T(8,128)S(1)} %get-tuple-element.70.early, f32[3,32,128]{2,1,0:T(8,128)S(1)} %get-tuple-element.71.late, f32[32,128]{1,0:T(8,128)S(1)} %collective-permute-done.6.from_low, ...), custom_call_target="tpu_custom_call" | custom-call | flops 2000000 | bytes 600000 | tf_op jit(solution)/shard_map/boundary_faces/pallas_call | solution.py:555
  (7 shorter events, 0.1 us)
Async XLA Ops:
  1.1 32.7 %collective-permute-start.6 = (f32[32,128]{1,0:T(8,128)S(1)}, f32[32,128]{1,0:T(8,128)S(1)}, u32[]{:S(2)}, u32[]{:S(2)}) collective-permute-start(f32[32,128]{1,0:T(8,128)S(1)} %get-tuple-element.72), channel_id=1, source_target_pairs={{448,512},{449,513},{450,514},{451,515},{452,516},{453,517},{454,5... | collective-permute-start | bytes 49160 | tf_op jit(solution)/shard_map/ppermute | solution.py:641
  3.1 10.2 %collective-permute-start = (f32[32,128]{1,0:T(8,128)S(1)}, f32[32,128]{1,0:T(8,128)}, u32[]{:S(2)}, u32[]{:S(2)}) collective-permute-start(f32[32,128]{1,0:T(8,128)S(1)} %get-tuple-element.25), channel_id=1, source_target_pairs={{1,2},{2,1},{3,4},{4,3},{5,6},{6,5},{7,8},{8,7},{9,10},{10,9},{11,... | collective-permute-start | bytes 49160 | tf_op jit(solution)/shard_map/cond/branch_1_fun/ppermute | solution.py:620
  11.4 5.7 %collective-permute-start.1 = (f32[32,128]{1,0:T(8,128)S(1)}, f32[32,128]{1,0:T(8,128)}, u32[]{:S(2)}, u32[]{:S(2)}) collective-permute-start(f32[32,128]{1,0:T(8,128)S(1)} %get-tuple-element.26), channel_id=1, source_target_pairs={{0,64},{64,0},{1,65},{65,1},{2,66},{66,2},{3,67},{67,3},{4,68},{68... | collective-permute-start | bytes 49160 | tf_op jit(solution)/shard_map/cond/branch_1_fun/ppermute | solution.py:620
  17.1 16.7 %collective-permute-start.7 = (f32[32,128]{1,0:T(8,128)S(1)}, f32[32,128]{1,0:T(8,128)S(1)}, u32[]{:S(2)}, u32[]{:S(2)}) collective-permute-start(f32[32,128]{1,0:T(8,128)S(1)} %get-tuple-element.73), channel_id=1, source_target_pairs={{512,448},{513,449},{514,450},{515,451},{516,452},{517,453},{518,4... | collective-permute-start | bytes 49160 | tf_op jit(solution)/shard_map/ppermute | solution.py:641

commit v5 on v4

--- a/solution.py
+++ b/solution.py
@@ -11,6 +11,7 @@
 
 CHUNK = 16
 TILE = 64
+RESIDENT = (0, 2, 3, 6)
 GROUP = 8
 WRAP = 8
 FIRST, SECOND = "first", "second"
@@ -129,24 +130,32 @@
     return jnp.concatenate(pieces, axis=0)
 
 
-def pack_kernel(n_x, n_y, air, edge_map, own, late_even, wrap, row_even, col_even, col_odd, back, maps, sems):
+def pack_kernel(n_x, n_y, air_in, edge_map, *refs):
+    fetched, refs = refs[: len(RESIDENT) - 1], refs[len(RESIDENT) - 1 :]
+    air, *targets = refs[: len(RESIDENT)]
+    own, late_even, wrap, row_even, col_even, col_odd, back, maps, sems = refs[len(RESIDENT) :]
     rows, cols, _ = air.shape
     row, col = lax.axis_index("gx"), lax.axis_index("gy")
     west, east = (row + n_x - 1) % n_x, (row + 1) % n_x
     south, north = (col + n_y - 1) % n_y, (col + 1) % n_y
     copies = [
-        pltpu.make_async_copy(air.at[:, 0], own.at[2], sems.at[0]),
-        pltpu.make_async_copy(air.at[:, cols - 1], own.at[3], sems.at[1]),
-        pltpu.make_async_copy(air.at[0], own.at[0], sems.at[2]),
-        pltpu.make_async_copy(air.at[rows - 1], own.at[1], sems.at[3]),
-        pltpu.make_async_copy(edge_map.at[west], maps.at[0], sems.at[4]),
-        pltpu.make_async_copy(edge_map.at[row], maps.at[1], sems.at[5]),
-        pltpu.make_async_copy(edge_map.at[east], maps.at[2], sems.at[6]),
+        pltpu.make_async_copy(air_in, air, sems.at[0]),
+        pltpu.make_async_copy(edge_map.at[west], maps.at[0], sems.at[1]),
+        pltpu.make_async_copy(edge_map.at[row], maps.at[1], sems.at[2]),
+        pltpu.make_async_copy(edge_map.at[east], maps.at[2], sems.at[3]),
     ]
-    for copy in copies:
+    later = [
+        pltpu.make_async_copy(source, target, sems.at[4 + k])
+        for k, (source, target) in enumerate(zip(fetched, targets))
+    ]
+    for copy in copies + later:
         copy.start()
     for copy in copies:
         copy.wait()
+    own[0] = air[0]
+    own[1] = air[rows - 1]
+    own[2] = air[:, 0, :]
+    own[3] = air[:, cols - 1, :]
 
     def asked(code):
         edge = own[code % 4]
@@ -166,6 +175,8 @@
     col_even[...] = paired
     beside = (row % WRAP == 0) | (row % WRAP == WRAP - 1)
     wrap[...] = jnp.where(beside, odd, paired)
+    for copy in later:
+        copy.wait()
     col_odd[...] = jnp.where(even, to_south, to_north)
 
 
@@ -177,12 +188,13 @@
 
     @pl.when(ahead(row, col) == early)
     def _():
-        copies = []
+        copies = {}
         for k, (source, target) in enumerate(zip(inputs, held)):
             if k == 1:
                 source = source.at[row]
-            copies.append(pltpu.make_async_copy(source, target, sems.at[k]))
-        for k in (0, 2, 3, 6, 1, 7, 8, 4, 5, 9):
+            if k not in RESIDENT:
+                copies[k] = pltpu.make_async_copy(source, target, sems.at[k])
+        for k in (1, 7, 8, 4, 5, 9):
             copies[k].start()
 
         def ready(*numbers):
@@ -231,8 +243,6 @@
     rows, cols, feat = air.shape
     tiles = rows * cols // TILE
     chunk_cols = CHUNK * cols
-
-    ready(0, 2, 3, 6)
 
     def base_chunk(c, carry):
         start = pl.multiple_of(c * CHUNK, CHUNK)
@@ -434,21 +444,23 @@
     return pltpu.with_memory_space_constraint(x, pltpu.VMEM)
 
 
-def packed(air_state, edge_map, n_x, n_y):
-    rows, cols, feat = air_state.shape
+def packed(inputs, edge_map, n_x, n_y):
+    rows, cols, feat = inputs[0].shape
+    first = [inputs[k] for k in RESIDENT]
     return pl.pallas_call(
         functools.partial(pack_kernel, n_x, n_y),
-        out_shape=[vmem_array((4, cols, feat), jnp.float32)]
+        out_shape=[vmem_array(x.shape, x.dtype) for x in first]
+        + [vmem_array((4, cols, feat), jnp.float32)]
         + [vmem_array((cols, feat), jnp.float32)] * 6,
-        in_specs=[in_hbm()] * 2,
-        out_specs=[in_vmem()] * 7,
+        in_specs=[in_hbm()] * (1 + len(first)),
+        out_specs=[in_vmem()] * (7 + len(first)),
         scratch_shapes=[
             pltpu.SMEM((3,) + edge_map.shape[1:], jnp.int32),
-            pltpu.SemaphoreType.DMA((7,)),
+            pltpu.SemaphoreType.DMA((3 + len(first),)),
         ],
         compiler_params=pltpu.CompilerParams(vmem_limit_bytes=4 * 1024 * 1024),
         name="own_edges",
-    )(kept_in_hbm(air_state), kept_in_hbm(edge_map))
+    )(*map(kept_in_hbm, (first[0], edge_map, *first[1:])))
 
 
 def idle_kernel(*refs):
@@ -475,8 +487,9 @@
     air_state = inputs[0]
     held = []
     for k, x in enumerate(inputs):
-        space = pltpu.SMEM if k == 1 else pltpu.VMEM
-        held.append(space(x.shape[1:] if k == 1 else x.shape, x.dtype))
+        if k not in RESIDENT:
+            space = pltpu.SMEM if k == 1 else pltpu.VMEM
+            held.append(space(x.shape[1:] if k == 1 else x.shape, x.dtype))
     like = lambda x: vmem_array(x.shape, x.dtype)
     outs = [vmem_array(air_state.shape, jnp.float32)]
     outs += [like(x) for x in started[1:]]
@@ -502,12 +515,14 @@
         for (arrays, wanted, _), target in zip(groups, targets):
             moved.append((refs[at : at + len(arrays)], results[target], wanted))
             at += len(arrays)
-        main_kernel(early, refs[:n_in], moved, results[0], (rest[:n_in], *rest[n_in:]))
+        own = iter(rest)
+        every_input = [refs[k] if k in RESIDENT else next(own) for k in range(n_in)]
+        main_kernel(early, refs[:n_in], moved, results[0], (every_input, *own))
 
     return pl.pallas_call(
         kernel,
         out_shape=outs + [like(x) for x in passed],
-        in_specs=[in_hbm()] * n_in
+        in_specs=[in_vmem() if k in RESIDENT else in_hbm() for k in range(n_in)]
         + [in_vmem()] * (n_passed + n_started)
         + [anywhere()] * len(every),
         out_specs=[in_vmem()] * (n_fixed + n_passed),
@@ -526,7 +541,11 @@
             flops=1_000_000_000, bytes_accessed=4_200_000, transcendentals=1_000_000
         ),
         name="columns_ahead" if early else "columns_behind",
-    )(*map(kept_in_hbm, inputs), *map(kept_in_vmem, (*passed, *started)), *every)
+    )(
+        *(kept_in_vmem(x) if k in RESIDENT else kept_in_hbm(x) for k, x in enumerate(inputs)),
+        *map(kept_in_vmem, (*passed, *started)),
+        *every,
+    )
 
 
 def collected(arrays, wanted, passed):
@@ -645,9 +664,11 @@
     is_first = lambda r: r % WRAP == 0
     is_middle = lambda r: (r % WRAP > 0) & (r % WRAP < WRAP - 1)
     is_late = lambda r: r % WRAP >= WRAP - 2
-    own, late_even, wrap, row_even, col_even, col_odd, back = packed(
-        air_state, edge_map.transpose(0, 2, 1), n_x, n_y
-    )
+    *first_inputs, own, late_even, wrap, row_even, col_even, col_odd, back = packed(
+        inputs, edge_map.transpose(0, 2, 1), n_x, n_y
+    )
+    resident = dict(zip(RESIDENT, first_inputs))
+    inputs = tuple(resident.get(k, x) for k, x in enumerate(inputs))
     partial, wrap, row_even, col_even, col_odd, back = interior(
         True, inputs, (wrap, row_even, col_even, col_odd, back)
     )

time: 35.4 us -> 33.9 us (0.958); the launches traced: 34.9 us -> 33.9 us
  Pallas kernels: 12.1 us -> 11 us
    pallas_call x2, Pallas kernels: 9.93 us -> 8.63 us  [interior(): pl.pallas_call(kernel, out_shape=outs + [like(x) for x in passed], in_spe...]
  transfers between devices with their start and end apart: 4 -> 4, of which waited for: 1 -> 1; matrix products, arithmetic and copies ran while one was open for 0% -> 0% of each run, Pallas kernels for 28% -> 25%
where the time goes in v5:
time: 33.9 us
  starting transfers between devices  18.9 us (56%)
  Pallas kernels  11 us (32%)
  waiting for transfers between devices  3.81 us (11%)
    ppermute x2, starting transfers between devices, move(): return lax.ppermute(x, ('gx', 'gy'), swap(rows, cols, n_y))  10.2 us
    ppermute x2, starting transfers between devices, across(): return lax.ppermute(x, ('gx', 'gy'), pairs + swap(others, cols, n_y))  8.69 us
    pallas_call x2, Pallas kernels, interior(): pl.pallas_call(kernel, out_shape=outs + [like(x) for x in passed], in_spe...  8.63 us
    ppermute x2, waiting for transfers between devices, move(): return lax.ppermute(x, ('gx', 'gy'), swap(rows, cols, n_y))  3.8 us
    pallas_call x1, Pallas kernels, packed(): pl.pallas_call(functools.partial(pack_kernel, n_x, n_y), out_shape=[vmem_...  1.26 us
    pallas_call x1, Pallas kernels, boundary(): pl.pallas_call(edge_kernel, out_shape=jax.ShapeDtypeStruct(partial.shape,...  1.13 us
  transfers between devices with their start and end apart: 4, of which 1 were waited for; matrix products, arithmetic and copies ran while one was open for 0% of the time, Pallas kernels for 25%

profile of v5, /device:TPU:384, one launch (start us, length us, event | category | flops | bytes accessed | tf_op | source)
XLA Modules:
  0.0 33.9 jit_solution(3255578579296411994)
XLA Ops:
  0.0 1.3 %own_edges.1 = (f32[32,32,128]{2,1,0:T(8,128)S(1)}, bf16[128,1024]{1,0:T(8,128)(2,1)S(1)}, f32[1,1024]{1,0:T(1,128)S(1)}, bf16[1024,128]{1,0:T(8,128)(2,1)S(1)},...) custom-call(f32[32,32,128]{2,1,0:T(8,128)} %air_in.1, ...), custom_call_target="tpu_custom_call" | custom-call | tf_op jit(solution)/shard_map/own_edges/pallas_call | solution.py:450
  1.3 0.1 columns_ahead.1
  1.4 1.9 %collective-permute-start.6 = (f32[32,128]{1,0:T(8,128)S(1)}, f32[32,128]{1,0:T(8,128)S(1)}, u32[]{:S(2)}, u32[]{:S(2)}) collective-permute-start(f32[32,128]{1,0:T(8,128)S(1)} %get-tuple-element.80), channel_id=1, source_target_pairs={{448,512},{449,513},{450,514},{451,515},{452,516},{453,517},{454,5... | collective-permute-start | bytes 49160 | tf_op jit(solution)/shard_map/ppermute | solution.py:660
  3.4 14.0 %conditional.4 = ((f32[32,128]{1,0:T(8,128)}, f32[32,128]{1,0:T(8,128)})) conditional(s32[]{:T(128)} %convert_element_type.12, f32[32,128]{1,0:T(8,128)S(1)} %get-tuple-element.67, (f32[32,128]{1,0:T(8,128)S(1)}, f32[32,128]{1,0:T(8,128)S(1)}) %tuple.31), branch_computations={%region_0.1_spmd, %region_1.2_spmd} | conditional | bytes 131176 | solution.py:677
  3.4 8.3 %collective-permute-start = (f32[32,128]{1,0:T(8,128)S(1)}, f32[32,128]{1,0:T(8,128)}, u32[]{:S(2)}, u32[]{:S(2)}) collective-permute-start(f32[32,128]{1,0:T(8,128)S(1)} %get-tuple-element.25), channel_id=1, source_target_pairs={{1,2},{2,1},{3,4},{4,3},{5,6},{6,5},{7,8},{8,7},{9,10},{10,9},{11,... | collective-permute-start | bytes 49160 | tf_op jit(solution)/shard_map/cond/branch_1_fun/ppermute | solution.py:639
  11.6 1.9 %collective-permute-start.1 = (f32[32,128]{1,0:T(8,128)S(1)}, f32[32,128]{1,0:T(8,128)}, u32[]{:S(2)}, u32[]{:S(2)}) collective-permute-start(f32[32,128]{1,0:T(8,128)S(1)} %get-tuple-element.26), channel_id=1, source_target_pairs={{0,64},{64,0},{1,65},{65,1},{2,66},{66,2},{3,67},{67,3},{4,68},{68... | collective-permute-start | bytes 49160 | tf_op jit(solution)/shard_map/cond/branch_1_fun/ppermute | solution.py:639
  13.6 0.0 collective-permute-done
  13.6 3.8 %collective-permute-done.1 = f32[32,128]{1,0:T(8,128)} collective-permute-done((f32[32,128]{1,0:T(8,128)S(1)}, f32[32,128]{1,0:T(8,128)}, u32[]{:S(2)}, u32[]{:S(2)}) %collective-permute-start.1) | collective-permute-done | bytes 16416 | tf_op jit(solution)/shard_map/cond/branch_1_fun/ppermute | solution.py:639
  17.4 6.8 %collective-permute-start.7 = (f32[32,128]{1,0:T(8,128)S(1)}, f32[32,128]{1,0:T(8,128)S(1)}, u32[]{:S(2)}, u32[]{:S(2)}) collective-permute-start(f32[32,128]{1,0:T(8,128)S(1)} %get-tuple-element.81), channel_id=1, source_target_pairs={{512,448},{513,449},{514,450},{515,451},{516,452},{517,453},{518,4... | collective-permute-start | bytes 49160 | tf_op jit(solution)/shard_map/ppermute | solution.py:660
  24.3 8.5 %columns_behind.1 = (f32[32,32,128]{2,1,0:T(8,128)S(1)}, f32[3,32,128]{2,1,0:T(8,128)S(1)}, f32[3,32,128]{2,1,0:T(8,128)S(1)}) custom-call(f32[32,32,128]{2,1,0:T(8,128)S(1)} %get-tuple-element.57.refs_0_, s32[16,1,16]{2,1,0:T(1,128)} %refs_1_.3, bf16[128,1024]{1,0:T(8,128)(2,1)S(1)} %get-tuple-element.58.refs_2_, ...), custom_call_target="tpu_custom_call", output_to_operand_aliasing={{0}: (10, {}), {1}: (11, {})} | custom-call | flops 1000000000 | bytes 4200000 | tf_op jit(solution)/shard_map/columns_behind/pallas_call | solution.py:522
  32.8 0.0 collective-permute-done.6.from_low
  32.8 0.0 collective-permute-done.7.from_high
  32.8 1.1 %boundary_faces.1 = f32[32,32,128]{2,1,0:T(8,128)} custom-call(f32[4,32,128]{2,1,0:T(8,128)S(1)} %get-tuple-element.56.edges, f32[3,32,128]{2,1,0:T(8,128)S(1)} %get-tuple-element.78.early, f32[3,32,128]{2,1,0:T(8,128)S(1)} %get-tuple-element.79.late, f32[32,128]{1,0:T(8,128)S(1)} %collective-permute-done.6.from_low, ...), custom_call_target="tpu_custom_call" | custom-call | flops 2000000 | bytes 600000 | tf_op jit(solution)/shard_map/boundary_faces/pallas_call | solution.py:574
  (7 shorter events, 0.1 us)
Async XLA Ops:
  1.4 31.4 %collective-permute-start.6 = (f32[32,128]{1,0:T(8,128)S(1)}, f32[32,128]{1,0:T(8,128)S(1)}, u32[]{:S(2)}, u32[]{:S(2)}) collective-permute-start(f32[32,128]{1,0:T(8,128)S(1)} %get-tuple-element.80), channel_id=1, source_target_pairs={{448,512},{449,513},{450,514},{451,515},{452,516},{453,517},{454,5... | collective-permute-start | bytes 49160 | tf_op jit(solution)/shard_map/ppermute | solution.py:660
  3.4 10.2 %collective-permute-start = (f32[32,128]{1,0:T(8,128)S(1)}, f32[32,128]{1,0:T(8,128)}, u32[]{:S(2)}, u32[]{:S(2)}) collective-permute-start(f32[32,128]{1,0:T(8,128)S(1)} %get-tuple-element.25), channel_id=1, source_target_pairs={{1,2},{2,1},{3,4},{4,3},{5,6},{6,5},{7,8},{8,7},{9,10},{10,9},{11,... | collective-permute-start | bytes 49160 | tf_op jit(solution)/shard_map/cond/branch_1_fun/ppermute | solution.py:639
  11.6 5.7 %collective-permute-start.1 = (f32[32,128]{1,0:T(8,128)S(1)}, f32[32,128]{1,0:T(8,128)}, u32[]{:S(2)}, u32[]{:S(2)}) collective-permute-start(f32[32,128]{1,0:T(8,128)S(1)} %get-tuple-element.26), channel_id=1, source_target_pairs={{0,64},{64,0},{1,65},{65,1},{2,66},{66,2},{3,67},{67,3},{4,68},{68... | collective-permute-start | bytes 49160 | tf_op jit(solution)/shard_map/cond/branch_1_fun/ppermute | solution.py:639
  17.4 15.4 %collective-permute-start.7 = (f32[32,128]{1,0:T(8,128)S(1)}, f32[32,128]{1,0:T(8,128)S(1)}, u32[]{:S(2)}, u32[]{:S(2)}) collective-permute-start(f32[32,128]{1,0:T(8,128)S(1)} %get-tuple-element.81), channel_id=1, source_target_pairs={{512,448},{513,449},{514,450},{515,451},{516,452},{517,453},{518,4... | collective-permute-start | bytes 49160 | tf_op jit(solution)/shard_map/ppermute | solution.py:660

commit v6 on v5

--- a/solution.py
+++ b/solution.py
@@ -368,8 +368,9 @@
     lax.fori_loop(0, count, element, (zero,) * 4)
 
 
-def edge_kernel(edges, early, late, from_low, from_high, partial, out, low, high, top, bottom, sems):
-    col_odd_a, row_even_a, col_even_first = (early[k] for k in range(3))
+def edge_kernel(edges, outside, early, late, from_low, from_high, partial, out, low, high, top, bottom, sems):
+    col_odd_a, col_even_first = (early[k] for k in range(2))
+    row_even_a = outside[...]
     col_even_b, col_odd_b, row_even_b = (late[k] for k in range(3))
     rows, cols, feat = out.shape
     first, middle, final = pl.ds(0, 8), pl.ds(8, cols - 16), pl.ds(cols - 8, 8)
@@ -569,12 +570,12 @@
     )(*arrays, *map(kept_in_vmem, passed))
 
 
-def boundary(edges, early, late, from_low, from_high, partial):
+def boundary(edges, outside, early, late, from_low, from_high, partial):
     rows, cols, feat = partial.shape
     return pl.pallas_call(
         edge_kernel,
         out_shape=jax.ShapeDtypeStruct(partial.shape, jnp.float32),
-        in_specs=[in_vmem()] * 6,
+        in_specs=[in_vmem()] * 7,
         out_specs=in_hbm(),
         scratch_shapes=[
             pltpu.VMEM((rows, 8, feat), jnp.float32),
@@ -586,7 +587,7 @@
         compiler_params=pltpu.CompilerParams(vmem_limit_bytes=8 * 1024 * 1024),
         cost_estimate=pl.CostEstimate(flops=2_000_000, bytes_accessed=600_000, transcendentals=0),
         name="boundary_faces",
-    )(edges, early, late, from_low, from_high, partial)
+    )(edges, outside, early, late, from_low, from_high, partial)
 
 
 def swap(rows, cols, n_y):
@@ -638,12 +639,8 @@
     def move(x, rows, cols):
         return lax.ppermute(x, ("gx", "gy"), swap(rows, cols, n_y))
 
-    def exchange_early(col_odd, row_even):
-        same = [(i, i) for i in early]
-        return (
-            move(col_odd, same, col_odds),
-            move(row_even, [p for p in evens if p[1] not in late], col_same),
-        )
+    def exchange_early(col_odd):
+        return (move(col_odd, [(i, i) for i in early], col_odds),)
 
     def exchange_first(col_even):
         return (move(col_even, [(i, i) for i in first], col_evens),)
@@ -674,8 +671,9 @@
     )
     from_low = across(wrap, wraps, [(i, i) for i in inner], col_evens)
     first_traces = lax.cond(place == 0, exchange_first, nothing(1), col_even)
-    early_traces = lax.cond(place < WRAP - 1, exchange_early, nothing(2), col_odd, row_even)
+    early_traces = lax.cond(place < WRAP - 1, exchange_early, nothing(1), col_odd)
     early_traces = (*early_traces, *first_traces)
+    outside = move(row_even, [p for p in evens if p[1] not in late], col_same)
     early_held, back, late_even = collected(early_traces, is_first, (back, late_even))
     from_high = across(
         back, [(b, a) for a, b in wraps], [p for p in odds if p[0] not in late], col_same
@@ -691,7 +689,7 @@
         (partial, early_held),
         ((early_traces, is_middle, 1), ((*late_cols, *late_rows), is_late, None)),
     )
-    return boundary(own, early_held, late_held, from_low, from_high, partial)
+    return boundary(own, outside, early_held, late_held, from_low, from_high, partial)
 
 
 def solution(mesh):

time: 33.9 us -> 35.8 us (1.056)
  the two profiles are of different devices: /device:TPU:384 before, /device:TPU:256 now
where the time goes in v6:
time: 35.8 us; the launch traced here: 35.5 us
  starting transfers between devices  23.4 us (65%)
  Pallas kernels  10.3 us (29%)
  waiting for transfers between devices  1.52 us (4%)
    ppermute x2, starting transfers between devices, move(): return lax.ppermute(x, ('gx', 'gy'), swap(rows, cols, n_y))  13.5 us
    ppermute x2, starting transfers between devices, across(): return lax.ppermute(x, ('gx', 'gy'), pairs + swap(others, cols, n_y))  9.97 us
    pallas_call x2, Pallas kernels, interior(): pl.pallas_call(kernel, out_shape=outs + [like(x) for x in passed], in_spe...  7.87 us
    ppermute x2, waiting for transfers between devices, move(): return lax.ppermute(x, ('gx', 'gy'), swap(rows, cols, n_y))  1.52 us
    pallas_call x1, Pallas kernels, packed(): pl.pallas_call(functools.partial(pack_kernel, n_x, n_y), out_shape=[vmem_...  1.26 us
    pallas_call x1, Pallas kernels, boundary(): pl.pallas_call(edge_kernel, out_shape=jax.ShapeDtypeStruct(partial.shape,...  1.13 us
  transfers between devices with their start and end apart: 4, of which 1 were waited for; matrix products, arithmetic and copies ran while one was open for 0% of the time, Pallas kernels for 22%

profile of v6, /device:TPU:256, one launch (start us, length us, event | category | flops | bytes accessed | tf_op | source)
XLA Modules:
  0.0 35.5 jit_solution(6551749934149887060)
XLA Ops:
  0.0 1.3 %own_edges.1 = (f32[32,32,128]{2,1,0:T(8,128)S(1)}, bf16[128,1024]{1,0:T(8,128)(2,1)S(1)}, f32[1,1024]{1,0:T(1,128)S(1)}, bf16[1024,128]{1,0:T(8,128)(2,1)S(1)},...) custom-call(f32[32,32,128]{2,1,0:T(8,128)} %air_in.1, ...), custom_call_target="tpu_custom_call" | custom-call | tf_op jit(solution)/shard_map/own_edges/pallas_call | solution.py:451
  1.3 0.1 columns_ahead.1
  1.4 5.2 %collective-permute-start.5 = (f32[32,128]{1,0:T(8,128)S(1)}, f32[32,128]{1,0:T(8,128)S(1)}, u32[]{:S(2)}, u32[]{:S(2)}) collective-permute-start(f32[32,128]{1,0:T(8,128)S(1)} %get-tuple-element.62), channel_id=1, source_target_pairs={{0,64},{64,0},{1,65},{65,1},{2,66},{66,2},{3,67},{67,3},{4,68},{68... | collective-permute-start | bytes 49160 | tf_op jit(solution)/shard_map/ppermute | solution.py:640
  6.6 1.9 %collective-permute-start.6 = (f32[32,128]{1,0:T(8,128)S(1)}, f32[32,128]{1,0:T(8,128)S(1)}, u32[]{:S(2)}, u32[]{:S(2)}) collective-permute-start(f32[32,128]{1,0:T(8,128)S(1)} %get-tuple-element.74), channel_id=1, source_target_pairs={{448,512},{449,513},{450,514},{451,515},{452,516},{453,517},{454,5... | collective-permute-start | bytes 49160 | tf_op jit(solution)/shard_map/ppermute | solution.py:657
  8.6 9.8 %conditional.4 = (f32[32,128]{1,0:T(8,128)}) conditional(s32[]{:T(128)} %convert_element_type.12, f32[32,128]{1,0:T(8,128)S(1)} %get-tuple-element.64, f32[32,128]{1,0:T(8,128)S(1)} %get-tuple-element.64), branch_computations={%region_0.1_spmd, %region_1.2_spmd} | conditional | bytes 65584 | solution.py:674
  8.6 8.3 %collective-permute-start = (f32[32,128]{1,0:T(8,128)S(1)}, f32[32,128]{1,0:T(8,128)}, u32[]{:S(2)}, u32[]{:S(2)}) collective-permute-start(f32[32,128]{1,0:T(8,128)S(1)} %param.1), channel_id=1, source_target_pairs={{1,2},{2,1},{3,4},{4,3},{5,6},{6,5},{7,8},{8,7},{9,10},{10,9},{11,... | collective-permute-start | bytes 49160 | tf_op jit(solution)/shard_map/cond/branch_1_fun/ppermute | solution.py:640
  16.9 1.5 %collective-permute-done = f32[32,128]{1,0:T(8,128)} collective-permute-done((f32[32,128]{1,0:T(8,128)S(1)}, f32[32,128]{1,0:T(8,128)}, u32[]{:S(2)}, u32[]{:S(2)}) %collective-permute-start) | collective-permute-done | bytes 16416 | tf_op jit(solution)/shard_map/cond/branch_1_fun/ppermute | solution.py:640
  18.4 8.1 %collective-permute-start.7 = (f32[32,128]{1,0:T(8,128)S(1)}, f32[32,128]{1,0:T(8,128)S(1)}, u32[]{:S(2)}, u32[]{:S(2)}) collective-permute-start(f32[32,128]{1,0:T(8,128)S(1)} %get-tuple-element.75), channel_id=1, source_target_pairs={{512,448},{513,449},{514,450},{515,451},{516,452},{517,453},{518,4... | collective-permute-start | bytes 49160 | tf_op jit(solution)/shard_map/ppermute | solution.py:657
  26.5 7.7 %columns_behind.1 = (f32[32,32,128]{2,1,0:T(8,128)S(1)}, f32[2,32,128]{2,1,0:T(8,128)S(1)}, f32[3,32,128]{2,1,0:T(8,128)S(1)}) custom-call(f32[32,32,128]{2,1,0:T(8,128)S(1)} %get-tuple-element.53.refs_0_, s32[16,1,16]{2,1,0:T(1,128)} %refs_1_.3, bf16[128,1024]{1,0:T(8,128)(2,1)S(1)} %get-tuple-element.54.refs_2_, ...), custom_call_target="tpu_custom_call", output_to_operand_aliasing={{0}: (10, {}), {1}: (11, {})} | custom-call | flops 1000000000 | bytes 4200000 | tf_op jit(solution)/shard_map/columns_behind/pallas_call | solution.py:523
  34.3 0.0 collective-permute-done.5.outside
  34.3 0.0 collective-permute-done.6.from_low
  34.3 0.0 collective-permute-done.7.from_high
  34.3 1.1 %boundary_faces.1 = f32[32,32,128]{2,1,0:T(8,128)} custom-call(f32[4,32,128]{2,1,0:T(8,128)S(1)} %get-tuple-element.52.edges, f32[32,128]{1,0:T(8,128)S(1)} %collective-permute-done.5.outside, f32[2,32,128]{2,1,0:T(8,128)S(1)} %get-tuple-element.72.early, f32[3,32,128]{2,1,0:T(8,128)S(1)} %get-tuple-element.73.late, ...), custom_call_target="tpu_custom_call" | custom-call | flops 2000000 | bytes 600000 | tf_op jit(solution)/shard_map/boundary_faces/pallas_call | solution.py:575
  (7 shorter events, 0.1 us)
Async XLA Ops:
  1.4 32.9 %collective-permute-start.5 = (f32[32,128]{1,0:T(8,128)S(1)}, f32[32,128]{1,0:T(8,128)S(1)}, u32[]{:S(2)}, u32[]{:S(2)}) collective-permute-start(f32[32,128]{1,0:T(8,128)S(1)} %get-tuple-element.62), channel_id=1, source_target_pairs={{0,64},{64,0},{1,65},{65,1},{2,66},{66,2},{3,67},{67,3},{4,68},{68... | collective-permute-start | bytes 49160 | tf_op jit(solution)/shard_map/ppermute | solution.py:640
  6.6 27.7 %collective-permute-start.6 = (f32[32,128]{1,0:T(8,128)S(1)}, f32[32,128]{1,0:T(8,128)S(1)}, u32[]{:S(2)}, u32[]{:S(2)}) collective-permute-start(f32[32,128]{1,0:T(8,128)S(1)} %get-tuple-element.74), channel_id=1, source_target_pairs={{448,512},{449,513},{450,514},{451,515},{452,516},{453,517},{454,5... | collective-permute-start | bytes 49160 | tf_op jit(solution)/shard_map/ppermute | solution.py:657
  8.6 9.8 %collective-permute-start = (f32[32,128]{1,0:T(8,128)S(1)}, f32[32,128]{1,0:T(8,128)}, u32[]{:S(2)}, u32[]{:S(2)}) collective-permute-start(f32[32,128]{1,0:T(8,128)S(1)} %param.1), channel_id=1, source_target_pairs={{1,2},{2,1},{3,4},{4,3},{5,6},{6,5},{7,8},{8,7},{9,10},{10,9},{11,... | collective-permute-start | bytes 49160 | tf_op jit(solution)/shard_map/cond/branch_1_fun/ppermute | solution.py:640
  18.4 15.9 %collective-permute-start.7 = (f32[32,128]{1,0:T(8,128)S(1)}, f32[32,128]{1,0:T(8,128)S(1)}, u32[]{:S(2)}, u32[]{:S(2)}) collective-permute-start(f32[32,128]{1,0:T(8,128)S(1)} %get-tuple-element.75), channel_id=1, source_target_pairs={{512,448},{513,449},{514,450},{515,451},{516,452},{517,453},{518,4... | collective-permute-start | bytes 49160 | tf_op jit(solution)/shard_map/ppermute | solution.py:657
